TPU v7x, 256 devices: a whole 4x4x8 slice. The times are simulated.
256 devices in a mesh: fsdp: 32 (over z, y_hi, core), sp: 8 (over x, y_lo).
Axes of the slice: x: 4, y: 4 (y_hi: 2, y_lo: 2; y = y_hi * 2 + y_lo), z: 8, core: 2. Of those that a mesh axis runs over, the one named last changes fastest.
Arguments:
- tokens_in: bfloat16 [32768, 4096], P(('fsdp', 'sp')), may hold values from -8 to 8
- queries: bfloat16 [32768, 5120], P(('fsdp', 'sp')), may hold values from -4000 to 4000
- kv_weight: bfloat16 [4096, 1024], P(('fsdp', 'sp')), may hold values from -0.4 to 0.4
- value_head_matrix: float32 [5120], P('sp'), may hold values from -5 to 5
- packed_episode_lengths: int32 [32, 4], P('fsdp'), may hold values from 1 to 512, 1024 in all within a row
- value_target_positions: int32 [32, 256], P('fsdp'), may hold values from 0 to 1023
- returns: float32 [32, 256], P('fsdp'), may hold values from -8 to 8
Outputs:
- query_grad: bfloat16 [32768, 5120], P(('fsdp', 'sp'))
- input_grad: bfloat16 [32768, 4096], P(('fsdp', 'sp'))
- kv_weight_grad: float32 [4096, 1024], P(('fsdp', 'sp'))
Inputs may be any that keep to these rules, and one draw needn't show every extreme that they name: `packed_episode_lengths`: each slab's lengths add up to 1024.
All inputs are finite; a program needn't handle non-finite values.
Results may differ from a plain program's by a relative error of at most 0.014.
Values may be sent and summed in bfloat16 or wider, within the bound.
A program may use at most 128 MiB of HBM per device.

v0:
```python
import math

import jax
import jax.numpy as jnp
from jax import lax
from jax.sharding import PartitionSpec as P

QUERY_HEAD_PART = 40
KEY_VALUE_HEADS = 4
HEAD_SIZE = 128


neg_fill = -1e30


def episode_index(lengths, slab_len):
    bounds = jnp.cumsum(lengths)
    places = lax.broadcasted_iota(jnp.int32, (slab_len, bounds.shape[0]), 0)
    return jnp.sum((places >= bounds[None, :]).astype(jnp.int32), axis=1)


def on_device(
    tokens_in,
    queries,
    kv_weight,
    value_head_matrix,
    packed_episode_lengths,
    value_target_positions,
    returns,
):
    sequence_parallel_count = lax.axis_size("sp")
    rows_local_part = tokens_in.shape[0]
    slab_len = rows_local_part * sequence_parallel_count
    repeat_key_value = max(sequence_parallel_count // KEY_VALUE_HEADS, 1)
    key_value_local = KEY_VALUE_HEADS * repeat_key_value // sequence_parallel_count
    group_local = QUERY_HEAD_PART // sequence_parallel_count // key_value_local
    key_value_width = key_value_local * HEAD_SIZE
    score_scale = 1.0 / math.sqrt(HEAD_SIZE)
    full_weight = lax.all_gather(kv_weight, ("fsdp", "sp"), axis=0, tiled=True)
    key_value_rows = jnp.dot(tokens_in, full_weight, preferred_element_type=jnp.float32).astype(
        jnp.bfloat16
    )
    key_parts = jnp.repeat(
        key_value_rows[:, : KEY_VALUE_HEADS * HEAD_SIZE].reshape(
            rows_local_part, KEY_VALUE_HEADS // key_value_local, key_value_width
        ),
        repeat_key_value,
        axis=1,
    )
    value_parts = jnp.repeat(
        key_value_rows[:, KEY_VALUE_HEADS * HEAD_SIZE :].reshape(
            rows_local_part, KEY_VALUE_HEADS // key_value_local, key_value_width
        ),
        repeat_key_value,
        axis=1,
    )
    kv_send = jnp.concatenate([key_parts, value_parts], axis=2).reshape(
        rows_local_part, sequence_parallel_count * 2 * key_value_width
    )
    query_heads, kv_heads = (
        lax.all_to_all(queries, "sp", split_axis=1, concat_axis=0, tiled=True),
        lax.all_to_all(kv_send, "sp", split_axis=1, concat_axis=0, tiled=True),
    )
    queries_h = query_heads.reshape(slab_len, key_value_local, group_local, HEAD_SIZE)
    keys_h = kv_heads[:, :key_value_width].reshape(slab_len, key_value_local, HEAD_SIZE)
    values_h = kv_heads[:, key_value_width:].reshape(slab_len, key_value_local, HEAD_SIZE)
    value_readout = value_head_matrix.reshape(key_value_local, group_local, HEAD_SIZE)
    episode = episode_index(packed_episode_lengths[0], slab_len)
    key_places = lax.broadcasted_iota(jnp.int32, (slab_len,), 0)
    block_len = min(512, slab_len)
    block_starts = jnp.arange(slab_len // block_len, dtype=jnp.int32) * block_len

    def block_scores(row_start):
        q_block = lax.dynamic_slice_in_dim(queries_h, row_start, block_len, 0)
        raw_scores = (
            jnp.einsum("qcgd,kcd->cgqk", q_block, keys_h, preferred_element_type=jnp.float32)
            * score_scale
        )
        row_episode = lax.dynamic_slice_in_dim(episode, row_start, block_len, 0)
        row_places = row_start + lax.broadcasted_iota(jnp.int32, (block_len,), 0)
        allowed = (row_episode[:, None] == episode[None, :]) & (
            key_places[None, :] <= row_places[:, None]
        )
        return (jnp.where(allowed[None, None], raw_scores, neg_fill), q_block)

    def forward_block(row_start):
        masked, q_block = block_scores(row_start)
        row_max = jnp.max(masked, axis=-1)
        weights = jnp.exp(masked - row_max[..., None])
        row_sum = jnp.sum(weights, axis=-1)
        prob_rows = weights / row_sum[..., None]
        attended = jnp.einsum(
            "cgqk,kcd->qcgd",
            prob_rows.astype(jnp.bfloat16),
            values_h,
            preferred_element_type=jnp.float32,
        )
        return (row_max, row_sum, jnp.sum(attended * value_readout[None], axis=-1))

    row_maxes, row_sums, head_blocks = lax.map(forward_block, block_starts)
    head_value = head_blocks.reshape(slab_len, key_value_local, group_local)
    target_hits = (value_target_positions[0][:, None] == key_places[None, :]).astype(jnp.float32)
    partial_est = jnp.sum(target_hits * jnp.sum(head_value, axis=(1, 2))[None, :], axis=1)
    estimate = lax.psum(partial_est, "sp")
    row_coef = jnp.sum(target_hits * (estimate - returns[0])[:, None], axis=0)
    grad_out = (row_coef[:, None, None, None] * value_readout[None]).astype(jnp.bfloat16)
    delta_all = row_coef[:, None, None] * head_value

    def backward_block(grad_carry, inputs):
        key_acc, value_acc = grad_carry
        row_start, row_max, row_sum = inputs
        masked, q_block = block_scores(row_start)
        prob_rows = jnp.exp(masked - row_max[..., None]) / row_sum[..., None]
        probs_low = prob_rows.astype(jnp.bfloat16)
        grad_block = lax.dynamic_slice_in_dim(grad_out, row_start, block_len, 0)
        delta_block = jnp.transpose(
            lax.dynamic_slice_in_dim(delta_all, row_start, block_len, 0), (1, 2, 0)
        )
        grad_probs = jnp.einsum(
            "qcgd,kcd->cgqk", grad_block, values_h, preferred_element_type=jnp.float32
        )
        grad_scores = (prob_rows * (grad_probs - delta_block[..., None])).astype(jnp.bfloat16)
        query_part = (
            jnp.einsum("cgqk,kcd->qcgd", grad_scores, keys_h, preferred_element_type=jnp.float32)
            * score_scale
        )
        key_acc = (
            key_acc
            + jnp.einsum("cgqk,qcgd->kcd", grad_scores, q_block, preferred_element_type=jnp.float32)
            * score_scale
        )
        value_acc = value_acc + jnp.einsum(
            "cgqk,qcgd->kcd", probs_low, grad_block, preferred_element_type=jnp.float32
        )
        return ((key_acc, value_acc), query_part.astype(jnp.bfloat16))

    zero_grads = (
        jnp.zeros((slab_len, key_value_local, HEAD_SIZE), jnp.float32),
        jnp.zeros((slab_len, key_value_local, HEAD_SIZE), jnp.float32),
    )
    (key_gradient, value_gradient), query_blocks = lax.scan(
        backward_block, zero_grads, (block_starts, row_maxes, row_sums)
    )
    query_grad = query_blocks.reshape(slab_len, key_value_local * group_local * HEAD_SIZE)
    kv_partial = jnp.concatenate(
        [
            key_gradient.reshape(slab_len, key_value_width),
            value_gradient.reshape(slab_len, key_value_width),
        ],
        axis=1,
    )
    query_seq = lax.all_to_all(query_grad, "sp", split_axis=0, concat_axis=1, tiled=True)
    kv_back = lax.all_to_all(kv_partial, "sp", split_axis=0, concat_axis=1, tiled=True)
    summed_total = jnp.sum(
        kv_back.reshape(
            rows_local_part,
            sequence_parallel_count // repeat_key_value,
            repeat_key_value,
            2,
            key_value_width,
        ),
        axis=2,
    )
    kv_seq = (
        jnp.transpose(summed_total, (0, 2, 1, 3))
        .reshape(rows_local_part, 2 * KEY_VALUE_HEADS * HEAD_SIZE)
        .astype(jnp.bfloat16)
    )
    weight_grad = lax.psum_scatter(
        lax.dot_general(
            tokens_in, kv_seq, (((0,), (0,)), ((), ())), preferred_element_type=jnp.float32
        ),
        ("fsdp", "sp"),
        scatter_dimension=0,
        tiled=True,
    )
    input_grad = lax.dot_general(
        kv_seq, full_weight, (((1,), (1,)), ((), ())), preferred_element_type=jnp.float32
    ).astype(jnp.bfloat16)
    return (query_seq, input_grad, weight_grad)


def solution(mesh):
    return jax.shard_map(
        on_device,
        mesh=mesh,
        in_specs=(
            P(("fsdp", "sp"), None),
            P(("fsdp", "sp"), None),
            P(("fsdp", "sp"), None),
            P("sp"),
            P("fsdp", None),
            P("fsdp", None),
            P("fsdp", None),
        ),
        out_specs=(P(("fsdp", "sp"), None), P(("fsdp", "sp"), None), P(("fsdp", "sp"), None)),
        check_vma=False,
    )
```

profile of v0, /device:TPU:1, one launch (start us, length us, event | category | flops | bytes accessed | tf_op | source)
XLA Modules:
  0.0 2166.9 jit_solution(9489608279096407157)
XLA Ops:
  7.9 2.4 copy.82
  10.3 5.9 all-to-all-start
  16.2 715.7 %all-gather.2.cloned.1.call-done = bf16[4096,1024]{1,0:T(8,128)(2,1)} async-done(((bf16[16,1024]{1,0:T(8,128)(2,1)}), bf16[4096,1024]{1,0:T(8,128)(2,1)}) %all-gather.2.cloned.1.call-update) | async-done | bytes 8388624 | tf_op jit(solution)/shard_map/all_gather | solution.py:39
  731.9 4.6 convolution_convert_fusion.1
  737.6 3.6 all-to-all-start.1
  741.6 1.9 copy.83
  743.5 3.2 reshape.337
  746.7 1.8 copy.89
  752.5 25.6 %while.30 = (s32[]{:T(128)}, f32[2,1,5,512]{3,2,1,0:T(8,128)S(1)}, f32[2,1,5,512]{3,2,1,0:T(8,128)S(1)}, f32[2,512,1,5]{1,2,3,0:T(1,128)S(1)}, s32[2]{0:T(128)S(...) while((s32[]{:T(128)}, f32[2,1,5,512]{3,2,1,0:T(8,128)S(1)}, ...), condition=%wide.region_6.7_spmd.clone, body=%wide.region_2.6_spmd.clone.sunk | while | flops 1375855616 | bytes 35953380 | solution.py:100
  756.3 2.2 fusion.100
  758.6 3.0 fusion.101
  761.6 3.7 fusion.102
  769.1 2.2 fusion.100
  771.4 3.0 fusion.101
  774.3 3.7 fusion.102
  778.4 15.0 psum.7
  795.0 35.9 %while.31 = (s32[]{:T(128)}, f32[1024,1,128]{0,2,1:T(8,128)S(1)}, f32[1024,1,128]{0,2,1:T(8,128)}, bf16[2,512,1,5,128]{4,1,3,2,0:T(8,128)(2,1)}, s32[2]{0:T(128)...) while((s32[]{:T(128)}, f32[1024,1,128]{0,2,1:T(8,128)S(1)}, ...), condition=%wide.region_12.13_spmd.clone, body=%wide.region_11.12_spmd.clone.sunk | while | flops 3389784576 | bytes 75020672 | solution.py:141
  800.5 3.8 fusion.117
  804.3 4.3 fusion.115
  809.9 1.9 fusion.118
  818.4 3.8 fusion.117
  822.2 4.3 fusion.115
  827.9 1.9 fusion.118
  832.7 12.6 all_to_all.64
  845.6 8.0 convolution_bitcast_fusion.1
  853.7 17.5 copy.102
  871.2 3.5 copy.91
  876.3 2.6 copy.92
  878.9 3.6 all-to-all-start.2
  882.5 7.2 convolution_convert_fusion
  889.7 6.1 all-to-all-done.2
  897.2 1262.8 %reduce-scatter.4.cloned.1.call-done = f32[16,1024]{1,0:T(8,128)} async-done(((f32[4096,1024]{1,0:T(8,128)}), f32[16,1024]{1,0:T(8,128)}) %reduce-scatter.4.cloned.1.call-update) | async-done | bytes 65552
  (105 shorter events, 28.9 us)
Async XLA Ops:
  7.2 724.7 %copy-start = (bf16[128,4096]{1,0:T(8,128)(2,1)S(1)}, bf16[128,4096]{1,0:T(8,128)(2,1)}, u32[]{:S(2)}) copy-start(bf16[128,4096]{1,0:T(8,128)(2,1)} %param.11) | copy-start | bytes 3145732
  7.2 724.7 %all-gather.2.cloned.1.call-start = ((), (), s32[]{:S(2)}) async-start(), calls=%async_computation.5 | async-start | bytes 8421376 | tf_op jit(solution)/shard_map/all_gather | solution.py:39
  10.3 727.2 %all-to-all-start = ((bf16[128,8,640]{0,2,1:T(8,128)(2,1)}), bf16[128,8,640]{0,2,1:T(8,128)(2,1)S(1)}, u32[]{:S(2)}, u32[]{:S(2)}) async-start(bf16[128,8,640]{0,2,1:T(8,128)(2,1)} %bitcast.285), calls=%async_computation | async-start | bytes 2621440 | tf_op jit(solution)/shard_map/all_to_all | solution.py:61
  16.2 725.1 %copy-start.11 = (s32[1,4]{1,0:T(1,128)S(1)}, s32[1,4]{1,0:T(1,128)}, u32[]{:S(2)}) copy-start(s32[1,4]{1,0:T(1,128)} %param.15) | copy-start | bytes 52
  737.5 15.0 copy-start.8
  737.6 12.3 all-to-all-start.1
  741.2 1418.9 %reduce-scatter.4.cloned.1.call-start = ((), (), s32[]{:S(2)}) async-start(), calls=%async_computation.6 | async-start | bytes 16842752
  749.8 0.8 copy-start.1
  752.5 25.6 %copy-start.9 = (s32[1,256]{1,0:T(1,128)S(1)}, s32[1,256]{1,0:T(1,128)}, u32[]{:S(2)}) copy-start(s32[1,256]{1,0:T(1,128)} %param.16) | copy-start | bytes 3076
  752.5 40.9 %copy-start.10 = (f32[1,256]{1,0:T(1,128)S(1)}, f32[1,256]{1,0:T(1,128)}, u32[]{:S(2)}) copy-start(f32[1,256]{1,0:T(1,128)} %param.17) | copy-start | bytes 3076
  758.6 3.0 copy-start.7
  771.4 3.0 copy-start.7
  798.9 1.6 copy-start.4
  798.9 1.6 copy-start.5
  804.3 4.3 copy-start.6
  808.6 1.3 copy-start.2
  811.8 1.1 copy-start.3
  816.8 1.6 copy-start.4
  816.8 1.6 copy-start.5
  822.2 4.3 copy-start.6
  826.6 1.3 copy-start.2
  829.8 1.1 copy-start.3
  878.9 16.9 all-to-all-start.2
Sparse Core Ops, SparseCore 0:
  9.9 721.9 all-gather.1
  871.3 1288.7 reduce-scatter.3
where the time goes:
time: 2180 us; the launch traced here: 2170 us
  waiting for transfers between devices  1990 us (91%)
  matrix products  56.8 us (3%)
  local copies, waits for them, and re-layouts  46.7 us (2%)
  blocking collectives  27.6 us (1%)
    unnamed x3, waiting for transfers between devices  1260 us
    all_gather x1, waiting for transfers between devices, on_device(): full_weight = lax.all_gather(kv_weight, ('fsdp', 'sp'), axis=0, tiled=True)  716 us
  transfers between devices with their start and end apart: 5, of which 4 were waited for; matrix products, arithmetic and copies ran while one was open for 1% of the time, Pallas kernels for 0%

commit v1 on v0

v1 whole, which is shorter than its diff:
```python
import math

import jax
import jax.numpy as jnp
from jax import lax
from jax.experimental import pallas as pl
from jax.experimental.pallas import tpu as pltpu
from jax.sharding import PartitionSpec as P

HEADS = 40
KV = 4
GROUP = 10
D = 128
SCALE = 1.0 / math.sqrt(D)
ROWS = 128
WIN = 640
TILE = 32
NEG = -1e30
HIGH = lax.Precision.HIGHEST


def tdot(a, b, precision=None):
    return lax.dot_general(
        a, b, (((0,), (0,)), ((), ())), precision=precision, preferred_element_type=jnp.float32
    )


def ndot(a, b):
    return lax.dot_general(a, b, (((1,), (1,)), ((), ())), preferred_element_type=jnp.float32)


def attention_kernel(
    base_ref, len_ref, pos_ref, ret_ref, q_ref, k_ref, u_ref, dq_ref, dk_ref, w_ref,
    qc, dqc, props, probs, heads,
):
    base = base_ref[0]
    rows = base + lax.broadcasted_iota(jnp.int32, (ROWS, 1), 0)
    hits = (rows == pos_ref[...]).astype(jnp.float32)
    count = jnp.sum(hits, axis=1, keepdims=True)
    total_ret = jnp.sum(hits * ret_ref[...], axis=1, keepdims=True)
    marked = (count > 0).astype(jnp.float32)
    tri = (
        lax.broadcasted_iota(jnp.int32, (ROWS, ROWS), 1)
        <= lax.broadcasted_iota(jnp.int32, (ROWS, ROWS), 0)
    ).astype(jnp.bfloat16)
    rank = jnp.dot(
        tri, jnp.broadcast_to(marked, (ROWS, D)).astype(jnp.bfloat16),
        preferred_element_type=jnp.float32,
    )
    n = jnp.sum(marked).astype(jnp.int32)
    slots = lax.broadcasted_iota(jnp.int32, (ROWS, ROWS), 1)
    pick = ((rank.astype(jnp.int32) - 1 == slots) & (marked > 0)).astype(jnp.float32)
    lane = lax.broadcasted_iota(jnp.int32, (ROWS, D), 1)
    b1 = len_ref[0, 0]
    b2 = b1 + len_ref[0, 1]
    b3 = b2 + len_ref[0, 2]
    start = jnp.where(rows >= b3, b3, jnp.where(rows >= b2, b2, jnp.where(rows >= b1, b1, 0)))
    fields = jnp.where(lane == 0, count, 0.0)
    fields = jnp.where(lane == 1, total_ret, fields)
    fields = jnp.where(lane == 2, rows.astype(jnp.float32), fields)
    fields = jnp.where(lane == 3, start.astype(jnp.float32), fields)
    props[...] = tdot(pick, fields, HIGH)
    pick_low = pick.astype(jnp.bfloat16)
    qc[...] = tdot(pick_low, q_ref[...]).astype(jnp.bfloat16)
    dqc[...] = jnp.zeros_like(dqc)
    dk_ref[...] = jnp.zeros_like(dk_ref)
    w_ref[...] = jnp.zeros_like(w_ref)
    places = (base - 512) + lax.broadcasted_iota(jnp.int32, (1, WIN), 1)

    @pl.loop(0, (n + TILE - 1) // TILE)
    def _(t):
        at = pl.ds(pl.multiple_of(t * TILE, TILE), TILE)
        prop = props[at, :]
        cnt, ret = prop[:, 0:1], prop[:, 1:2]
        row, low = prop[:, 2:3].astype(jnp.int32), prop[:, 3:4].astype(jnp.int32)
        allowed = (places >= low) & (places <= row)
        estimate = jnp.zeros((TILE, 1), jnp.float32)
        for c in range(KV):
            keys = k_ref[:, c * D : (c + 1) * D]
            q = jnp.concatenate(
                [qc[at, (c * GROUP + g) * D : (c * GROUP + g + 1) * D] for g in range(GROUP)], axis=0
            )
            scores = ndot(q, keys) * SCALE
            for g in range(GROUP):
                h = c * GROUP + g
                s = jnp.where(allowed, scores[g * TILE : (g + 1) * TILE, :], NEG)
                e = jnp.exp(s - jnp.max(s, axis=1, keepdims=True))
                p = e / jnp.sum(e, axis=1, keepdims=True)
                probs[h] = p
                low_p = p.astype(jnp.bfloat16).astype(jnp.float32)
                hv = jnp.sum(low_p * u_ref[h : h + 1, :], axis=1, keepdims=True)
                heads[h] = hv
                estimate = estimate + hv
        coef = cnt * estimate - ret
        for c in range(KV):
            keys = k_ref[:, c * D : (c + 1) * D]
            q = jnp.concatenate(
                [qc[at, (c * GROUP + g) * D : (c * GROUP + g + 1) * D] for g in range(GROUP)], axis=0
            )
            parts = []
            for g in range(GROUP):
                h = c * GROUP + g
                p = probs[h]
                low_p = p.astype(jnp.bfloat16).astype(jnp.float32)
                w_ref[h : h + 1, :] += jnp.sum(low_p * coef, axis=0, keepdims=True)
                parts.append(
                    (p * (coef * u_ref[h : h + 1, :] - coef * heads[h])).astype(jnp.bfloat16)
                )
            gs = jnp.concatenate(parts, axis=0)
            dq = (jnp.dot(gs, keys, preferred_element_type=jnp.float32) * SCALE).astype(jnp.bfloat16)
            for g in range(GROUP):
                h = c * GROUP + g
                dqc[at, h * D : (h + 1) * D] = dq[g * TILE : (g + 1) * TILE, :]
            dk_ref[:, c * D : (c + 1) * D] += tdot(gs, q) * SCALE

    dq_ref[...] = jnp.dot(
        pick_low, dqc[...], preferred_element_type=jnp.float32
    ).astype(jnp.bfloat16)


def attention(base, lengths, positions, returns, queries, keys, u):
    vmem = pl.BlockSpec(memory_space=pltpu.VMEM)
    smem = pl.BlockSpec(memory_space=pltpu.SMEM)
    return pl.pallas_call(
        attention_kernel,
        out_shape=(
            jax.ShapeDtypeStruct((ROWS, HEADS * D), jnp.bfloat16),
            jax.ShapeDtypeStruct((WIN, KV * D), jnp.float32),
            jax.ShapeDtypeStruct((HEADS, WIN), jnp.float32),
        ),
        in_specs=[smem, smem, vmem, vmem, vmem, vmem, vmem],
        out_specs=(vmem, vmem, vmem),
        scratch_shapes=[
            pltpu.VMEM((ROWS, HEADS * D), jnp.bfloat16),
            pltpu.VMEM((ROWS, HEADS * D), jnp.bfloat16),
            pltpu.VMEM((ROWS, D), jnp.float32),
            pltpu.VMEM((HEADS, TILE, WIN), jnp.float32),
            pltpu.VMEM((HEADS, TILE, 1), jnp.float32),
        ],
        compiler_params=pltpu.CompilerParams(vmem_limit_bytes=48 * 2**20),
    )(base, lengths, positions, returns, queries, keys, u)


def block_diagonal(vhm):
    head_kv = lax.broadcasted_iota(jnp.int32, (HEADS, KV, 1), 0) // GROUP
    kv = lax.broadcasted_iota(jnp.int32, (HEADS, KV, 1), 1)
    return jnp.where(head_kv == kv, vhm.reshape(HEADS, 1, D), 0.0).reshape(HEADS, KV * D)


def split(x):
    hi = x.astype(jnp.bfloat16)
    return hi, (x - hi.astype(jnp.float32)).astype(jnp.bfloat16)


def on_device(tokens, queries, kv_weight, vhm, lengths, positions, returns):
    sp = lax.axis_index("sp")
    base = sp * ROWS
    readout = block_diagonal(lax.all_gather(vhm, "sp", axis=0, tiled=True))
    wv = kv_weight[:, KV * D :].astype(jnp.float32)
    folded = lax.dot_general(
        wv, readout, (((1,), (1,)), ((), ())), precision=HIGH, preferred_element_type=jnp.float32
    )
    hi, lo = split(folded)
    mine = jnp.concatenate(
        [kv_weight[:, : KV * D], hi, lo, jnp.zeros((hi.shape[0], D - 2 * HEADS), jnp.bfloat16)], axis=1
    )
    weight = lax.all_gather(mine, ("fsdp", "sp"), axis=0, tiled=True)
    rows = jnp.dot(tokens, weight, preferred_element_type=jnp.float32)
    k_mine = rows[:, : KV * D].astype(jnp.bfloat16)
    u_mine = (rows[:, 512:552] + rows[:, 552:592]).T
    k_all = jnp.pad(lax.all_gather(k_mine, "sp", axis=0, tiled=True), ((512, 0), (0, 0)))
    u_all = jnp.pad(lax.all_gather(u_mine, "sp", axis=1, tiled=True), ((0, 0), (512, 0)))
    k_win = lax.dynamic_slice_in_dim(k_all, base, WIN, 0)
    u_win = lax.dynamic_slice_in_dim(u_all, base, WIN, 1)
    dq, dk, w = attention(base.reshape(1), lengths, positions, returns, queries, k_win, u_win)
    part = jnp.concatenate([dk, w.T], axis=1)
    whole = lax.dynamic_update_slice_in_dim(
        jnp.zeros((1536, 552), jnp.float32), part, base, 0
    )[512:]
    grad = lax.psum_scatter(whole, "sp", scatter_dimension=0, tiled=True)
    k_grad = grad[:, :512].astype(jnp.bfloat16)
    w_hi, w_lo = split(grad[:, 512:])
    pad = jnp.zeros((ROWS, D - 3 * HEADS), jnp.bfloat16)
    left = jnp.concatenate([k_grad, w_hi, w_lo, w_hi, pad], axis=1)
    right = jnp.concatenate([weight[:, :552], weight[:, 512:592], weight[:, 592:600]], axis=1)
    input_grad = lax.dot_general(
        left, right, (((1,), (1,)), ((), ())), preferred_element_type=jnp.float32
    ).astype(jnp.bfloat16)
    outer = tdot(tokens, left[:, :592])
    outer = jnp.concatenate([outer[:, :512], outer[:, 512:552] + outer[:, 552:592]], axis=1)
    mine_grad = lax.psum_scatter(outer, ("fsdp", "sp"), scatter_dimension=0, tiled=True)
    v_grad = jnp.dot(
        mine_grad[:, 512:], readout, precision=HIGH, preferred_element_type=jnp.float32
    )
    return dq, input_grad, jnp.concatenate([mine_grad[:, :512], v_grad], axis=1)


def solution(mesh):
    rows = P(("fsdp", "sp"), None)
    slab = P("fsdp", None)
    return jax.shard_map(
        on_device,
        mesh=mesh,
        in_specs=(rows, rows, rows, P("sp"), slab, slab, slab),
        out_specs=(rows, rows, rows),
        check_vma=False,
    )
```

time: 2180 us -> 2210 us (1.014)
  waiting for transfers between devices: 1990 us -> 2080 us
  matrix products: 56.8 us -> 12.5 us
    reduce_scatter x0 -> x1, waiting for transfers between devices: none -> 70 us  [on_device(): grad = lax.psum_scatter(whole, 'sp', scatter_dimension=0, tiled=True)]
    all_gather x0 -> x2, blocking collectives: none -> 44.7 us  [the longest x1 22.4 us: on_device(): readout = block_diagonal(lax.all_gather(vhm, 'sp', axis=0, tiled=True))]
    dot_general x17 -> x5, matrix products: 56.8 us -> 12.5 us  [the longest x1 5.28 us: on_device(): lax.dot_general(left, right, (((1,), (1,)), ((), ())), preferred_element_...]
    all_gather x1 -> x2, waiting for transfers between devices: 716 us -> 741 us  [the longest x1 722 us: on_device(): weight = lax.all_gather(mine, ('fsdp', 'sp'), axis=0, tiled=True)]
    unnamed x3 -> x5, waiting for transfers between devices: 1260 us -> 1270 us
  transfers between devices with their start and end apart: 5 -> 4, of which waited for: 4 -> 4; matrix products, arithmetic and copies ran while one was open for 1% -> 0% of each run, Pallas kernels for 0% -> 0%
where the time goes in v1:
time: 2210 us; the launch traced here: 2190 us
  waiting for transfers between devices  2080 us (94%)
  blocking collectives  44.7 us (2%)
  local copies, waits for them, and re-layouts  27 us (1%)
    unnamed x5, waiting for transfers between devices  1270 us
    all_gather x1, waiting for transfers between devices, on_device(): weight = lax.all_gather(mine, ('fsdp', 'sp'), axis=0, tiled=True)  722 us
    reduce_scatter x1, waiting for transfers between devices, on_device(): grad = lax.psum_scatter(whole, 'sp', scatter_dimension=0, tiled=True)  70 us
  transfers between devices with their start and end apart: 4, of which 4 were waited for; matrix products, arithmetic and copies ran while one was open for 0% of the time, Pallas kernels for 0%

profile of v1, /device:TPU:1, one launch (start us, length us, event | category | flops | bytes accessed | tf_op | source)
XLA Modules:
  0.0 2193.3 jit_solution(11051885516722015396)
XLA Ops:
  7.3 0.8 reshape.70
  8.0 0.7 slice.51
  8.7 22.4 %all-gather = f32[8,1,640]{2,1,0:T(1,128)S(1)} all-gather(f32[1,1,640]{2,1,0:T(1,128)S(1)} %reshape.70), channel_id=1, replica_groups=mesh['fsdp'=32,'sp'=8] {'sp'}, dimensions={0}, use_global_device_ids=true | all-gather | bytes 23040 | tf_op jit(solution)/shard_map/all_gather | solution.py:158
  31.4 0.8 subtract_convert_fusion.1
  32.3 0.7 maximum_maximum_fusion
  33.1 721.9 %all-gather.4.cloned.1.call-done = bf16[4096,640]{1,0:T(8,128)(2,1)} async-done(((bf16[16,640]{1,0:T(8,128)(2,1)}), bf16[4096,640]{1,0:T(8,128)(2,1)}) %all-gather.4.cloned.1.call-update) | async-done | bytes 5242896 | tf_op jit(solution)/shard_map/all_gather | solution.py:167
  755.1 4.0 convolution_bitcast_fusion.1
  759.1 0.7 slice.94
  759.9 22.3 %all_gather.15 = f32[40,1024]{1,0:T(8,128)S(1)} all-gather(f32[40,128]{1,0:T(8,128)S(1)} %fusion.17), channel_id=1, replica_groups=mesh['fsdp'=32,'sp'=8] {'sp'}, dimensions={1}, use_global_device_ids=true | all-gather | bytes 184320 | tf_op jit(solution)/shard_map/all_gather | solution.py:172
  782.1 18.9 all-gather.6.cloned.1.call-done
  801.0 1.8 pad_dynamic-slice_fusion
  802.8 1.3 copy.14.k_ref
  804.2 6.9 shard_map.94
  811.1 1.1 copy-done.2
  812.2 0.2 copy.15
  812.4 0.3 broadcast_in_dim.36
  812.6 0.9 copy-done.3
  813.6 1.7 slice.69
  815.3 0.2 reduce-scatter.7.cloned.1.call-start
  815.6 70.0 %reduce-scatter.5.cloned.1.call-done = f32[128,552]{1,0:T(8,128)} async-done(((f32[1024,552]{1,0:T(8,128)}), f32[128,552]{1,0:T(8,128)}) %reduce-scatter.5.cloned.1.call-update) | async-done | bytes 282640 | tf_op jit(solution)/shard_map/reduce_scatter | solution.py:180
  885.5 0.9 subtract_convert_fusion
  886.5 1.0 slice.93
  887.4 1.4 convolution_bitcast_fusion
  889.0 3.8 slice.74
  892.7 8.0 pad_maximum_fusion
  900.7 10.5 copy.17
  911.2 1.3 slice.73
  912.7 5.3 fusion.4
  918.0 1266.5 %reduce-scatter.7.cloned.1.call-done = f32[16,552]{1,0:T(8,128)} async-done(((f32[4096,552]{1,0:T(8,128)}), f32[16,552]{1,0:T(8,128)}) %reduce-scatter.7.cloned.1.call-update) | async-done | bytes 35344
  2184.5 0.9 fusion.12
  2185.3 0.8 slice.77
  2186.1 0.6 pad_maximum_fusion.1
  (31 shorter events, 0.9 us)
Async XLA Ops:
  7.2 747.9 %copy-start = (bf16[128,4096]{1,0:T(8,128)(2,1)S(1)}, bf16[128,4096]{1,0:T(8,128)(2,1)}, u32[]{:S(2)}) copy-start(bf16[128,4096]{1,0:T(8,128)(2,1)} %param.7) | copy-start | bytes 3145732
  7.2 747.9 %all-gather.4.cloned.1.call-start = ((), (), s32[]{:S(2)}) async-start(), calls=%async_computation.2 | async-start | bytes 5263360 | tf_op jit(solution)/shard_map/all_gather | solution.py:167
  33.0 771.1 %copy-start.1 = (bf16[128,5120]{1,0:T(8,128)(2,1)S(1)}, bf16[128,5120]{1,0:T(8,128)(2,1)}, u32[]{:S(2)}) copy-start(bf16[128,5120]{1,0:T(8,128)(2,1)} %q_ref.1) | copy-start | bytes 3932164
  33.1 771.1 %copy-start.4 = (s32[1,256]{1,0:T(1,128)S(1)}, s32[1,256]{1,0:T(1,128)}, u32[]{:S(2)}) copy-start(s32[1,256]{1,0:T(1,128)} %pos_ref.1) | copy-start | bytes 3076
  33.1 771.1 %copy-start.5 = (f32[1,256]{1,0:T(1,128)S(1)}, f32[1,256]{1,0:T(1,128)}, u32[]{:S(2)}) copy-start(f32[1,256]{1,0:T(1,128)} %ret_ref.1) | copy-start | bytes 3076
  33.1 771.1 %copy-start.6 = (s32[1,4]{1,0:T(1,128)S(1)}, s32[1,4]{1,0:T(1,128)}, u32[]{:S(2)}) copy-start(s32[1,4]{1,0:T(1,128)} %len_ref.1) | copy-start | bytes 52
  33.1 767.9 %all-gather.6.cloned.1.call-start = ((), (), s32[]{:S(2)}) async-start(), calls=%async_computation.3 | async-start | bytes 1179648 | tf_op jit(solution)/shard_map/all_gather | solution.py:171
  759.8 125.7 %reduce-scatter.5.cloned.1.call-start = ((), (), s32[]{:S(2)}) async-start(), calls=%async_computation.4 | async-start | bytes 2949120 | tf_op jit(solution)/shard_map/reduce_scatter | solution.py:180
  811.1 1.1 copy-start.2
  812.2 1.3 copy-start.3
  815.3 1369.1 %reduce-scatter.7.cloned.1.call-start = ((), (), s32[]{:S(2)}) async-start(), calls=%async_computation.5 | async-start | bytes 10526720
Sparse Core Ops, SparseCore 0:
  33.2 721.8 all-gather.3
  759.9 41.0 all-gather.5
  815.5 70.0 reduce-scatter.4
  911.4 1273.0 reduce-scatter.6

commit v2 on v1

v2 whole, which is shorter than its diff:
```python
import math

import jax
import jax.numpy as jnp
from jax import lax
from jax.experimental import pallas as pl
from jax.experimental.pallas import tpu as pltpu
from jax.sharding import PartitionSpec as P

HEADS = 40
KV = 4
GROUP = 10
D = 128
SCALE = 1.0 / math.sqrt(D)
ROWS = 128
WIN = 640
TILE = 32
NEG = -1e30
HIGH = lax.Precision.HIGHEST


def tdot(a, b, precision=None):
    return lax.dot_general(
        a, b, (((0,), (0,)), ((), ())), precision=precision, preferred_element_type=jnp.float32
    )


def ndot(a, b):
    return lax.dot_general(a, b, (((1,), (1,)), ((), ())), preferred_element_type=jnp.float32)


def attention_kernel(
    len_ref, pos_ref, ret_ref, q_ref, k_ref, vhm_ref, dq_ref, far_ref, near_ref, w_ref,
    qc, dqc, props, probs, heads, dk_ref, u_ref,
):
    base = lax.axis_index("sp") * ROWS
    rows = base + lax.broadcasted_iota(jnp.int32, (ROWS, 1), 0)
    hits = (rows == pos_ref[...]).astype(jnp.float32)
    count = jnp.sum(hits, axis=1, keepdims=True)
    total_ret = jnp.sum(hits * ret_ref[...], axis=1, keepdims=True)
    marked = (count > 0).astype(jnp.float32)
    tri = (
        lax.broadcasted_iota(jnp.int32, (ROWS, ROWS), 1)
        <= lax.broadcasted_iota(jnp.int32, (ROWS, ROWS), 0)
    ).astype(jnp.bfloat16)
    rank = jnp.dot(
        tri, jnp.broadcast_to(marked, (ROWS, D)).astype(jnp.bfloat16),
        preferred_element_type=jnp.float32,
    )
    n = jnp.sum(marked).astype(jnp.int32)
    slots = lax.broadcasted_iota(jnp.int32, (ROWS, ROWS), 1)
    pick = ((rank.astype(jnp.int32) - 1 == slots) & (marked > 0)).astype(jnp.float32)
    lane = lax.broadcasted_iota(jnp.int32, (ROWS, D), 1)
    b1 = len_ref[0, 0]
    b2 = b1 + len_ref[0, 1]
    b3 = b2 + len_ref[0, 2]
    start = jnp.where(rows >= b3, b3, jnp.where(rows >= b2, b2, jnp.where(rows >= b1, b1, 0)))
    fields = jnp.where(lane == 0, count, 0.0)
    fields = jnp.where(lane == 1, total_ret, fields)
    fields = jnp.where(lane == 2, rows.astype(jnp.float32), fields)
    fields = jnp.where(lane == 3, start.astype(jnp.float32), fields)
    props[...] = tdot(pick, fields, HIGH)
    pick_low = pick.astype(jnp.bfloat16)
    qc[...] = tdot(pick_low, q_ref[...]).astype(jnp.bfloat16)
    dqc[...] = jnp.zeros_like(dqc)
    dk_ref[...] = jnp.zeros_like(dk_ref)
    w_ref[...] = jnp.zeros_like(w_ref)
    for c in range(KV):
        readout = jnp.concatenate(
            [vhm_ref[h // 5, h % 5 : h % 5 + 1, :] for h in range(c * GROUP, (c + 1) * GROUP)]
            + [jnp.zeros((6, D), jnp.float32)], axis=0,
        )
        high = readout.astype(jnp.bfloat16)
        rest = readout - high.astype(jnp.float32)
        mid = rest.astype(jnp.bfloat16)
        low = (rest - mid.astype(jnp.float32)).astype(jnp.bfloat16)
        values = k_ref[:, (KV + c) * D : (KV + c + 1) * D]
        u_ref[c] = ndot(high, values) + (ndot(mid, values) + ndot(low, values))
    places = (base - 512) + lax.broadcasted_iota(jnp.int32, (1, WIN), 1)

    @pl.loop(0, (n + TILE - 1) // TILE)
    def _(t):
        at = pl.ds(pl.multiple_of(t * TILE, TILE), TILE)
        prop = props[at, :]
        cnt, ret = prop[:, 0:1], prop[:, 1:2]
        row, low = prop[:, 2:3].astype(jnp.int32), prop[:, 3:4].astype(jnp.int32)
        allowed = (places >= low) & (places <= row)
        estimate = jnp.zeros((TILE, 1), jnp.float32)
        for c in range(KV):
            keys = k_ref[:, c * D : (c + 1) * D]
            q = jnp.concatenate(
                [qc[at, (c * GROUP + g) * D : (c * GROUP + g + 1) * D] for g in range(GROUP)], axis=0
            )
            scores = ndot(q, keys) * SCALE
            for g in range(GROUP):
                h = c * GROUP + g
                s = jnp.where(allowed, scores[g * TILE : (g + 1) * TILE, :], NEG)
                e = jnp.exp(s - jnp.max(s, axis=1, keepdims=True))
                p = e / jnp.sum(e, axis=1, keepdims=True)
                probs[h] = p
                low_p = p.astype(jnp.bfloat16).astype(jnp.float32)
                hv = jnp.sum(low_p * u_ref[c, g : g + 1, :], axis=1, keepdims=True)
                heads[h] = hv
                estimate = estimate + hv
        coef = cnt * estimate - ret
        for c in range(KV):
            keys = k_ref[:, c * D : (c + 1) * D]
            q = jnp.concatenate(
                [qc[at, (c * GROUP + g) * D : (c * GROUP + g + 1) * D] for g in range(GROUP)], axis=0
            )
            values = k_ref[:, (KV + c) * D : (KV + c + 1) * D]
            grad_out = jnp.concatenate(
                [
                    (coef * vhm_ref[h // 5, h % 5 : h % 5 + 1, :]).astype(jnp.bfloat16)
                    for h in range(c * GROUP, (c + 1) * GROUP)
                ],
                axis=0,
            )
            grad_probs = ndot(grad_out, values)
            parts = []
            for g in range(GROUP):
                h = c * GROUP + g
                p = probs[h]
                low_p = p.astype(jnp.bfloat16).astype(jnp.float32)
                w_ref[h : h + 1, :] += jnp.sum(low_p * coef, axis=0, keepdims=True)
                grad_p = grad_probs[g * TILE : (g + 1) * TILE, :]
                parts.append((p * (grad_p - coef * heads[h])).astype(jnp.bfloat16))
            gs = jnp.concatenate(parts, axis=0)
            dq = (jnp.dot(gs, keys, preferred_element_type=jnp.float32) * SCALE).astype(jnp.bfloat16)
            for g in range(GROUP):
                h = c * GROUP + g
                dqc[at, h * D : (h + 1) * D] = dq[g * TILE : (g + 1) * TILE, :]
            dk_ref[:, c * D : (c + 1) * D] += tdot(gs, q) * SCALE

    far_ref[...] = dk_ref[: WIN - ROWS, :].astype(jnp.bfloat16)
    near_ref[...] = dk_ref[WIN - ROWS :, :]
    dq_ref[...] = jnp.dot(
        pick_low, dqc[...], preferred_element_type=jnp.float32
    ).astype(jnp.bfloat16)


VMEM = pl.BlockSpec(memory_space=pltpu.VMEM)
SMEM = pl.BlockSpec(memory_space=pltpu.SMEM)


def shape(dims, kind=jnp.bfloat16):
    return jax.ShapeDtypeStruct(dims, kind)


def attention(lengths, positions, returns, queries, keys, vhm):
    return pl.pallas_call(
        attention_kernel,
        out_shape=(
            shape((ROWS, HEADS * D)),
            shape((WIN - ROWS, KV * D)),
            shape((ROWS, KV * D), jnp.float32),
            shape((HEADS, WIN), jnp.float32),
        ),
        in_specs=[SMEM] + [VMEM] * 5,
        out_specs=(VMEM,) * 4,
        scratch_shapes=[
            pltpu.VMEM((ROWS, HEADS * D), jnp.bfloat16),
            pltpu.VMEM((ROWS, HEADS * D), jnp.bfloat16),
            pltpu.VMEM((ROWS, D), jnp.float32),
            pltpu.VMEM((HEADS, TILE, WIN), jnp.float32),
            pltpu.VMEM((HEADS, TILE, 1), jnp.float32),
            pltpu.VMEM((WIN, KV * D), jnp.float32),
            pltpu.VMEM((KV, 16, WIN), jnp.float32),
        ],
        compiler_params=pltpu.CompilerParams(vmem_limit_bytes=48 * 2**20),
    )(lengths, positions, returns, queries, keys, vhm)


MESH = pl.DeviceIdType.MESH
Z, YH, X, YL = 8, 2, 4, 2
Y = YH * YL
SP = X * YL
BACK = 4


class Place:
    def __init__(self):
        fsdp, self.sp = lax.axis_index("fsdp"), lax.axis_index("sp")
        self.core = fsdp % 2
        self.yh = (fsdp // 2) % YH
        self.z = fsdp // 4
        self.x, self.yl = self.sp // YL, self.sp % YL
        self.y = self.yh * YL + self.yl

    def at(self, z=None, yh=None, core=None, x=None, yl=None):
        z = self.z if z is None else z
        yh = self.yh if yh is None else yh
        core = self.core if core is None else core
        x = self.x if x is None else x
        yl = self.yl if yl is None else yl
        return (z * 4 + yh * 2 + core, x * YL + yl)

    def partner(self):
        return self.at(core=1 - self.core)

    def along(self, axis, r):
        if axis == "x":
            x = (self.x + r) % X
            return self.at(x=x), x
        if axis == "z":
            z = (self.z + r) % Z
            return self.at(z=z), z
        y = (self.y + r) % Y
        return self.at(yh=y // YL, yl=y % YL), y

    def slab(self, r):
        return (lax.axis_index("fsdp"), (self.sp + r) % SP)


COUNT = {"x": X, "y": Y, "z": Z}


class Copies:
    def __init__(self, send, recv):
        self.send, self.recv, self.used, self.open = send, recv, 0, []

    def make(self, src, dst, to):
        i = self.used
        self.used += 1
        return pltpu.make_async_remote_copy(
            src_ref=src, dst_ref=dst, send_sem=self.send.at[i], recv_sem=self.recv.at[i],
            device_id=to, device_id_type=MESH,
        )

    def start(self, src, dst, to):
        copy = self.make(src, dst, to)
        copy.start()
        self.open.append(copy)
        return copy

    def close(self):
        for copy in self.open:
            copy.wait_send()


def greet(place):
    barrier = pltpu.get_barrier_semaphore()
    peers = [place.partner()]
    for axis in ("x", "y", "z"):
        peers += [place.along(axis, r)[0] for r in range(1, COUNT[axis])]
    peers += [place.at(x=(place.x + r) % X, yl=1 - place.yl) for r in range(1, X)]
    for peer in peers:
        pl.semaphore_signal(barrier, inc=1, device_id=peer, device_id_type=MESH)
    pl.semaphore_wait(barrier, len(peers))


def gather_kernel(
    t_ref, kv_ref, vhm_ref,
    kwin, vfull, wb, wg, wa, tb,
    tsend, pr, pin, ssem, rsem,
):
    place = Place()
    copies = Copies(ssem, rsem)
    z, yh, x, yl, core, j = place.z, place.yh, place.x, place.yl, place.core, place.sp
    other = 1 - core

    wb[z, yh, x, yl] = kv_ref[:, 0:384]
    wg[z, yh, x, yl] = kv_ref[:, 384:768]
    wa[z, yh, x, yl] = kv_ref[:, 768:1024]
    vfull[j] = vhm_ref[...]
    here = pl.ds(pl.multiple_of(core * ROWS, ROWS), ROWS)
    there = pl.ds(pl.multiple_of(other * ROWS, ROWS), ROWS)
    for b in range(16):
        mine = pl.ds(pl.multiple_of(b * 256 + core * 128, 128), 128)
        theirs = pl.ds(pl.multiple_of(b * 256 + other * 128, 128), 128)
        tb[here, b * 128 : (b + 1) * 128] = t_ref[:, mine]
        tsend[:, b * 128 : (b + 1) * 128] = t_ref[:, theirs]

    greet(place)

    def spread(axis, view):
        return [
            copies.start(view, view, place.along(axis, r)[0]) for r in range(1, COUNT[axis])
        ]

    def arrive(group):
        for copy in group:
            copy.wait_recv()

    b1 = spread("z", wb.at[z, yh, x, yl])
    g1 = spread("z", wg.at[z, yh, x, yl])
    a1 = spread("x", wa.at[z, yh, x, yl])
    v1 = [copies.start(vfull.at[j], vfull.at[j], place.slab(r)) for r in range(1, SP)]
    tswap = copies.start(tsend, tb.at[here, :], place.partner())

    arrive(b1)
    b2 = spread("y", wb.at[:, yh, x, yl])
    arrive(g1)
    g2 = spread("x", wg.at[:, yh, x, yl])
    arrive(a1)
    a2 = spread("y", wa.at[z, yh, :, yl])
    arrive(b2)
    b3 = spread("x", wb.at[:, :, x, :])
    arrive(g2)
    g3 = spread("y", wg.at[:, yh, :, yl])
    arrive(a2)
    a3 = spread("z", wa.at[z])
    arrive([tswap])
    arrive(b3)
    pr[:, 0:384] = jnp.dot(
        tb[...], wb[...].reshape(2048, 384), preferred_element_type=jnp.float32
    )
    arrive(g3)
    pr[:, 384:768] = jnp.dot(
        tb[...], wg[...].reshape(2048, 384), preferred_element_type=jnp.float32
    )
    arrive(a3)
    pr[:, 768:1024] = jnp.dot(
        tb[...], wa[...].reshape(2048, 256), preferred_element_type=jnp.float32
    )
    pswap = copies.start(pr.at[there, :], pin, place.partner())
    arrive([pswap])
    own = slice(WIN - ROWS, WIN)
    kwin[own, :] = (pr[here, :] + pin[...]).astype(jnp.bfloat16)
    moves = []
    for d in range(1, BACK + 1):
        slot = slice((BACK - d) * ROWS, (BACK - d + 1) * ROWS)
        moves.append(copies.make(kwin.at[own, :], kwin.at[slot, :], place.slab(d)))

        @pl.when(j + d < SP)
        def _():
            moves[-1].start()

        @pl.when(j - d < 0)
        def _():
            kwin[slot, :] = jnp.zeros((ROWS, 2 * KV * D), jnp.bfloat16)

    arrive(v1)
    for d in range(1, BACK + 1):

        @pl.when(j - d >= 0)
        def _():
            moves[d - 1].wait_recv()

        @pl.when(j + d < SP)
        def _():
            moves[d - 1].wait_send()

    copies.close()


def gather(tokens, kv_weight, vhm):
    f32 = jnp.float32
    return pl.pallas_call(
        gather_kernel,
        out_shape=(
            shape((WIN, 2 * KV * D)),
            shape((SP, 8, D), f32),
            shape((Z, YH, X, YL, 16, 384)),
            shape((Z, YH, X, YL, 16, 384)),
            shape((Z, YH, X, YL, 16, 256)),
            shape((2 * ROWS, 2048)),
        ),
        in_specs=[VMEM] * 3,
        out_specs=(VMEM,) * 6,
        scratch_shapes=[
            pltpu.VMEM((ROWS, 2048), jnp.bfloat16),
            pltpu.VMEM((2 * ROWS, 1024), f32),
            pltpu.VMEM((ROWS, 1024), f32),
            pltpu.SemaphoreType.DMA((64,)),
            pltpu.SemaphoreType.DMA((64,)),
        ],
        compiler_params=pltpu.CompilerParams(
            collective_id=0, has_side_effects=True, vmem_limit_bytes=48 * 2**20
        ),
    )(tokens, kv_weight, vhm)


def reduce_kernel(
    far_ref, near_ref, w_ref, wb, wg, wa, tb, vfull,
    ig_ref, wgrad_ref,
    readout, rk, rw, gk, gw, gb, pb, pg, pa,
    rb1, rb2, rb3, rg1, rg2, rg3, ra1, ra2, ra3,
    sb1, sb2, sg1, sg2, sa1, sa2, igs, igr, ssem, rsem,
):
    place = Place()
    copies = Copies(ssem, rsem)
    z, yh, x, yl, core, j = place.z, place.yh, place.x, place.yl, place.core, place.sp
    other = 1 - core
    f32 = jnp.float32
    here = pl.ds(pl.multiple_of(core * ROWS, ROWS), ROWS)
    there = pl.ds(pl.multiple_of(other * ROWS, ROWS), ROWS)
    greet(place)

    pairs = []
    for d in range(1, BACK + 1):
        slot = slice((BACK - d) * ROWS, (BACK - d + 1) * ROWS)
        pairs.append(
            (
                copies.make(far_ref.at[slot, :], rk.at[d - 1], place.slab(SP - d)),
                copies.make(w_ref.at[:, slot], rw.at[d - 1], place.slab(SP - d)),
            )
        )

        @pl.when(j - d >= 0)
        def _():
            for copy in pairs[-1]:
                copy.start()

    readout[...] = jnp.zeros_like(readout)
    for h in range(HEADS):
        c = h // GROUP
        readout[h : h + 1, c * D : (c + 1) * D] = vfull[h // 5, h % 5 : h % 5 + 1, :]
    gk[...] = near_ref[...]
    gw[...] = w_ref[:, WIN - ROWS :]
    for d in range(1, BACK + 1):

        @pl.when(j + d < SP)
        def _():
            for copy in pairs[d - 1]:
                copy.wait_recv()
            gk[...] += rk[d - 1].astype(f32)
            gw[...] += rw[d - 1]

    gb[here, 0:512] = gk[...].astype(jnp.bfloat16)
    whi = gw[...].astype(jnp.bfloat16).astype(f32)
    wlo = gw[...] - whi
    stacked = jnp.concatenate([whi, wlo, jnp.zeros((48, ROWS), f32)], axis=0)
    gb[here, 1024:1152] = stacked.T.astype(jnp.bfloat16)
    gb[here, 512:1024] = lax.dot_general(
        gw[...], readout[0:HEADS, :], (((0,), (0,)), ((), ())), precision=HIGH,
        preferred_element_type=f32,
    ).astype(jnp.bfloat16)
    gswap = copies.start(gb.at[here, :], gb.at[here, :], place.partner())
    gswap.wait_recv()

    def rest(axis):
        return range(1, COUNT[axis])

    def add_up(own, slots, n):
        total = own.astype(f32)
        for k in range(n):
            total = total + slots[k].astype(f32)
        return total

    for n in range(Z):
        part = tdot(tb[:, n * 256 : (n + 1) * 256], gb[:, 0:256])
        pb[n] = part.astype(jnp.bfloat16).reshape(YH, X, YL, 16, 256)
    b1 = []
    for r in rest("x"):
        to, at = place.along("x", r)
        b1.append(copies.start(pb.at[:, :, at], rb1.at[r - 1], to))
    for n in range(Z):
        part = tdot(tb[:, n * 256 : (n + 1) * 256], gb[:, 256:512])
        pg[n] = part.astype(jnp.bfloat16).reshape(YH, X, YL, 16, 256)
    g1 = []
    for r in rest("y"):
        to, at = place.along("y", r)
        g1.append(copies.start(pg.at[:, at // YL, :, at % YL], rg1.at[r - 1], to))
    for n in range(Z):
        part = tdot(tb[:, n * 256 : (n + 1) * 256], gb[:, 1024:1152])
        part = part + pltpu.roll(part, 128 - 40, 1)
        pa[n] = part.astype(jnp.bfloat16).reshape(YH, X, YL, 16, 128)
    a1 = []
    for r in rest("z"):
        to, at = place.along("z", r)
        a1.append(copies.start(pa.at[at], ra1.at[r - 1], to))

    for n in range(Z):
        part = ndot(gb[:, 0:384], wb[n].reshape(256, 384))
        part = part + ndot(gb[:, 384:768], wg[n].reshape(256, 384))
        part = part + ndot(gb[:, 768:1024], wa[n].reshape(256, 256))
        igs[:, n * 256 : (n + 1) * 256] = part.astype(jnp.bfloat16)
    iswap = copies.start(igs.at[there, :], igr, place.partner())

    for copy in b1:
        copy.wait_recv()
    sb1[...] = add_up(pb[:, :, x], rb1, X - 1).astype(jnp.bfloat16)
    b2 = []
    for r in rest("y"):
        to, at = place.along("y", r)
        b2.append(copies.start(sb1.at[:, at // YL, at % YL], rb2.at[r - 1], to))
    for copy in g1:
        copy.wait_recv()
    sg1[...] = add_up(pg[:, yh, :, yl], rg1, Y - 1).astype(jnp.bfloat16)
    g2 = []
    for r in rest("x"):
        to, at = place.along("x", r)
        g2.append(copies.start(sg1.at[:, at], rg2.at[r - 1], to))
    for copy in a1:
        copy.wait_recv()
    sa1[...] = add_up(pa[z], ra1, Z - 1).astype(jnp.bfloat16)
    a2 = []
    for r in rest("y"):
        to, at = place.along("y", r)
        a2.append(copies.start(sa1.at[at // YL, :, at % YL], ra2.at[r - 1], to))
    for copy in b2:
        copy.wait_recv()
    sb2[...] = add_up(sb1[:, yh, yl], rb2, Y - 1).astype(jnp.bfloat16)
    b3 = []
    for r in rest("z"):
        to, at = place.along("z", r)
        b3.append(copies.start(sb2.at[at], rb3.at[r - 1], to))
    for copy in g2:
        copy.wait_recv()
    sg2[...] = add_up(sg1[:, x], rg2, X - 1).astype(jnp.bfloat16)
    g3 = []
    for r in rest("z"):
        to, at = place.along("z", r)
        g3.append(copies.start(sg2.at[at], rg3.at[r - 1], to))
    for copy in a2:
        copy.wait_recv()
    sa2[...] = add_up(sa1[yh, :, yl], ra2, Y - 1).astype(jnp.bfloat16)
    a3 = []
    for r in rest("x"):
        to, at = place.along("x", r)
        a3.append(copies.start(sa2.at[at], ra3.at[r - 1], to))

    iswap.wait_recv()
    for b in range(16):
        block = slice(b * 128, (b + 1) * 128)
        mine = pl.ds(pl.multiple_of(b * 256 + core * 128, 128), 128)
        theirs = pl.ds(pl.multiple_of(b * 256 + other * 128, 128), 128)
        ig_ref[:, mine] = igs[here, block]
        ig_ref[:, theirs] = igr[:, block]
    for copy in b3:
        copy.wait_recv()
    wgrad_ref[:, 0:256] = add_up(sb2[z], rb3, Z - 1)
    for copy in g3:
        copy.wait_recv()
    wgrad_ref[:, 256:512] = add_up(sg2[z], rg3, Z - 1)
    for copy in a3:
        copy.wait_recv()
    last = add_up(sa2[x], ra3, X - 1)
    wgrad_ref[:, 512:1024] = jnp.dot(
        last, readout[...], precision=HIGH, preferred_element_type=f32
    )
    for d in range(1, BACK + 1):

        @pl.when(j - d >= 0)
        def _():
            for copy in pairs[d - 1]:
                copy.wait_send()

    copies.close()


def reduce(far, near, w, wb, wg, wa, tb, vfull):
    f32, low = jnp.float32, jnp.bfloat16
    return pl.pallas_call(
        reduce_kernel,
        out_shape=(shape((ROWS, 4096)), shape((16, 1024), f32)),
        in_specs=[VMEM] * 8,
        out_specs=(VMEM, VMEM),
        scratch_shapes=[
            pltpu.VMEM((128, KV * D), f32),
            pltpu.VMEM((BACK, ROWS, KV * D), low),
            pltpu.VMEM((BACK, HEADS, ROWS), f32),
            pltpu.VMEM((ROWS, KV * D), f32),
            pltpu.VMEM((HEADS, ROWS), f32),
            pltpu.VMEM((2 * ROWS, 1152), low),
            pltpu.VMEM((Z, YH, X, YL, 16, 256), low),
            pltpu.VMEM((Z, YH, X, YL, 16, 256), low),
            pltpu.VMEM((Z, YH, X, YL, 16, 128), low),
            pltpu.VMEM((X - 1, Z, YH, YL, 16, 256), low),
            pltpu.VMEM((Y - 1, Z, 16, 256), low),
            pltpu.VMEM((Z - 1, 16, 256), low),
            pltpu.VMEM((Y - 1, Z, X, 16, 256), low),
            pltpu.VMEM((X - 1, Z, 16, 256), low),
            pltpu.VMEM((Z - 1, 16, 256), low),
            pltpu.VMEM((Z - 1, YH, X, YL, 16, 128), low),
            pltpu.VMEM((Y - 1, X, 16, 128), low),
            pltpu.VMEM((X - 1, 16, 128), low),
            pltpu.VMEM((Z, YH, YL, 16, 256), low),
            pltpu.VMEM((Z, 16, 256), low),
            pltpu.VMEM((Z, X, 16, 256), low),
            pltpu.VMEM((Z, 16, 256), low),
            pltpu.VMEM((YH, X, YL, 16, 128), low),
            pltpu.VMEM((X, 16, 128), low),
            pltpu.VMEM((2 * ROWS, 2048), low),
            pltpu.VMEM((ROWS, 2048), low),
            pltpu.SemaphoreType.DMA((64,)),
            pltpu.SemaphoreType.DMA((64,)),
        ],
        compiler_params=pltpu.CompilerParams(
            collective_id=1, has_side_effects=True, vmem_limit_bytes=56 * 2**20
        ),
    )(far, near, w, wb, wg, wa, tb, vfull)


def on_device(tokens, queries, kv_weight, vhm, lengths, positions, returns):
    vhm = jnp.pad(vhm.reshape(HEADS // SP, D), ((0, 8 - HEADS // SP), (0, 0)))
    kwin, vfull, wb, wg, wa, tb = gather(tokens, kv_weight, vhm)
    dq, far, near, w = attention(lengths, positions, returns, queries, kwin, vfull)
    input_grad, weight_grad = reduce(far, near, w, wb, wg, wa, tb, vfull)
    return dq, input_grad, weight_grad


def solution(mesh):
    rows = P(("fsdp", "sp"), None)
    slab = P("fsdp", None)
    return jax.shard_map(
        on_device,
        mesh=mesh,
        in_specs=(rows, rows, rows, P("sp"), slab, slab, slab),
        out_specs=(rows, rows, rows),
        check_vma=False,
    )
```

time: 2210 us -> 154 us (0.07)
  waiting for transfers between devices: 2080 us -> 0 us
  Pallas kernels: 6.9 us -> 140 us
  blocking collectives: 44.7 us -> 0 us
    unnamed x5 -> x0, waiting for transfers between devices: 1270 us -> none
    all_gather x2 -> x0, waiting for transfers between devices: 741 us -> none  [the longest x1 722 us: on_device(): weight = lax.all_gather(mine, ('fsdp', 'sp'), axis=0, tiled=True)]
    pallas_call x1 -> x3, Pallas kernels: 6.9 us -> 140 us  [the longest x1 66.1 us: reduce(): pl.pallas_call(reduce_kernel, out_shape=(shape((ROWS, 4096)), shape((16,...]
    reduce_scatter x1 -> x0, waiting for transfers between devices: 70 us -> none  [on_device(): grad = lax.psum_scatter(whole, 'sp', scatter_dimension=0, tiled=True)]
    all_gather x2 -> x0, blocking collectives: 44.7 us -> none  [the longest x1 22.4 us: on_device(): readout = block_diagonal(lax.all_gather(vhm, 'sp', axis=0, tiled=True))]
  transfers between devices with their start and end apart: 4 -> 0, of which waited for: 4 -> 0; matrix products, arithmetic and copies ran while one was open for 0% -> 0% of each run, Pallas kernels for 0% -> 0%
where the time goes in v2:
time: 154 us; the launch traced here: 153 us
  Pallas kernels  140 us (91%)
  local copies, waits for them, and re-layouts  13 us (8%)
    pallas_call x1, Pallas kernels, reduce(): pl.pallas_call(reduce_kernel, out_shape=(shape((ROWS, 4096)), shape((16,...  66.1 us
    pallas_call x1, Pallas kernels, gather(): pl.pallas_call(gather_kernel, out_shape=(shape((WIN, 2 * KV * D)), shape(...  65.4 us
    unnamed x30, local copies, waits for them, and re-layouts  12.4 us
    pallas_call x1, Pallas kernels, attention(): pl.pallas_call(attention_kernel, out_shape=(shape((ROWS, HEADS * D)), sha...  8.05 us

profile of v2, /device:TPU:1, one launch (start us, length us, event | category | flops | bytes accessed | tf_op | source)
XLA Modules:
  0.0 153.3 jit_solution(866460921143056115)
XLA Ops:
  0.6 0.7 pad.4.vhm_ref
  1.3 0.0 copy-start.2
  1.3 1.2 copy-done.2
  2.5 0.0 copy-start.9
  2.5 0.8 copy-done.9
  3.3 65.4 %shard_map.94 = (bf16[640,1024]{1,0:T(8,128)(2,1)S(1)}, f32[8,8,128]{2,1,0:T(8,128)S(1)}, bf16[8,2,4,2,16,384]{5,4,3,2,1,0:T(8,128)(2,1)S(1)}, bf16[8,2,4,2,16,3...) custom-call(bf16[128,4096]{1,0:T(8,128)(2,1)S(1)} %copy-done.2, ...), custom_call_target="tpu_custom_call" | custom-call | tf_op jit(solution)/shard_map/pallas_call | solution.py:349
  68.7 0.0 copy-start
  68.7 1.1 copy-done
  69.9 0.0 copy-start.3
  69.9 0.0 copy-start.4
  69.9 0.0 copy-start.7
  69.9 0.0 copy-start.1
  69.9 2.1 %copy-done.1 = bf16[128,5120]{1,0:T(8,128)(2,1)S(1)} copy-done((bf16[128,5120]{1,0:T(8,128)(2,1)S(1)}, bf16[128,5120]{1,0:T(8,128)(2,1)}, u32[]{:S(2)}) %copy-start.1) | copy-done | bytes 1310744
  72.0 0.0 copy-start.10
  72.0 0.7 copy-done.10
  72.6 0.0 copy-start.11
  72.7 0.7 copy-done.11
  73.3 0.0 copy-start.12
  73.3 0.7 copy-done.12
  74.0 8.0 %shard_map.95 = (bf16[128,5120]{1,0:T(8,128)(2,1)}, bf16[512,512]{1,0:T(8,128)(2,1)S(1)}, f32[128,512]{1,0:T(8,128)S(1)}, f32[40,640]{1,0:T(8,128)S(1)}) custom-call(s32[1,4]{1,0:T(1,128)S(1)} %copy-done.12, s32[1,256]{1,0:T(1,128)S(1)} %copy-done.10, f32[1,256]{1,0:T(1,128)S(1)} %copy-done.11, bf16[128,5120]{1,0:T(8,128)(2,1)S(1)} %copy-done.1, ...), custom_call_target="tpu_custom_call" | custom-call | tf_op jit(solution)/shard_map/pallas_call | solution.py:151
  82.0 0.0 copy-done.3
  82.0 0.0 copy-done.4
  82.0 0.0 copy-done.7
  82.0 0.0 copy-start.5
  82.1 0.8 copy-done.5
  82.9 0.7 copy-done.6
  83.6 0.6 copy-done.8
  84.2 66.1 %shard_map.96 = (bf16[128,4096]{1,0:T(8,128)(2,1)}, f32[16,1024]{1,0:T(8,128)}) custom-call(bf16[512,512]{1,0:T(8,128)(2,1)} %copy-done.5, f32[128,512]{1,0:T(8,128)} %copy-done.6, f32[40,640]{1,0:T(8,128)} %copy-done.8, bf16[8,2,4,2,16,384]{5,4,3,2,1,0:T(8,128)(2,1)} %copy-done, bf16[8,2,4,2,16,384]{5,4,3,2,1,0:T(8,128)(2,1)} %get-tuple-element.22.wg, ...), custom_call_target="tpu_custom_call" | custom-call | tf_op jit(solution)/shard_map/pallas_call | solution.py:545
  150.3 0.0 copy-start.13
  150.3 2.3 %copy.12 = bf16[128,4096]{1,0:T(8,128)(2,1)} copy(bf16[128,4096]{1,0:T(8,128)(2,1)} %get-tuple-element.31) | data formatting | bytes 2097152
  152.7 0.0 copy-done.13
  152.7 0.6 copy.13
  (2 shorter events, 0.0 us)
Async XLA Ops:
  1.3 1.2 copy-start.2
  2.5 0.8 copy-start.9
  68.7 1.1 copy-start
  69.9 12.2 %copy-start.3 = (bf16[8,2,4,2,16,256]{5,4,3,2,1,0:T(8,128)(2,1)}, bf16[8,2,4,2,16,256]{5,4,3,2,1,0:T(8,128)(2,1)S(1)}, u32[]{:S(2)}) copy-start(bf16[8,2,4,2,16,256]{5,4,3,2,1,0:T(8,128)(2,1)S(1)} %get-tuple-element.23.wa) | copy-start | bytes 3145732
  69.9 12.2 %copy-start.4 = (bf16[256,2048]{1,0:T(8,128)(2,1)}, bf16[256,2048]{1,0:T(8,128)(2,1)S(1)}, u32[]{:S(2)}) copy-start(bf16[256,2048]{1,0:T(8,128)(2,1)S(1)} %get-tuple-element.24.tb) | copy-start | bytes 3145732
  69.9 12.2 %copy-start.7 = (f32[8,8,128]{2,1,0:T(8,128)}, f32[8,8,128]{2,1,0:T(8,128)S(1)}, u32[]{:S(2)}) copy-start(f32[8,8,128]{2,1,0:T(8,128)S(1)} %get-tuple-element.16.vhm_ref.vfull) | copy-start | bytes 98308
  69.9 2.1 %copy-start.1 = (bf16[128,5120]{1,0:T(8,128)(2,1)S(1)}, bf16[128,5120]{1,0:T(8,128)(2,1)}, u32[]{:S(2)}) copy-start(bf16[128,5120]{1,0:T(8,128)(2,1)} %q_ref.1) | copy-start | bytes 3932164
  72.0 0.7 copy-start.10
  72.6 0.7 copy-start.11
  73.3 0.7 copy-start.12
  82.0 0.8 copy-start.5
  82.9 0.7 copy-start.6
  83.6 0.6 copy-start.8
  150.3 2.3 %copy-start.13 = (f32[16,1024]{1,0:T(8,128)S(1)}, f32[16,1024]{1,0:T(8,128)}, u32[]{:S(2)}) copy-start(f32[16,1024]{1,0:T(8,128)} %get-tuple-element.32) | copy-start | bytes 196612

commit v3 on v2

--- a/solution.py
+++ b/solution.py
@@ -14,7 +14,8 @@
 SCALE = 1.0 / math.sqrt(D)
 ROWS = 128
 WIN = 640
-TILE = 32
+TILE = 48
+PADDED = 144
 NEG = -1e30
 HIGH = lax.Precision.HIGHEST
 
@@ -30,10 +31,27 @@
 
 
 def attention_kernel(
-    len_ref, pos_ref, ret_ref, q_ref, k_ref, vhm_ref, dq_ref, far_ref, near_ref, w_ref,
-    qc, dqc, props, probs, heads, dk_ref, u_ref,
+    len_hbm, pos_hbm, ret_hbm, q_hbm, k_hbm, v_hbm, vhm_hbm, dq_ref, far_hbm, near_hbm, w_hbm,
+    len_ref, pos_ref, ret_ref, q_ref, k_ref, v_ref, vhm_ref,
+    qc, dqc, props, probs, heads, dk_ref, u_ref, far_ref, w_ref, sems,
 ):
     base = lax.axis_index("sp") * ROWS
+    moves = [
+        pltpu.make_async_copy(src, dst, sems.at[i])
+        for i, (src, dst) in enumerate(
+            (
+                (len_hbm, len_ref), (pos_hbm, pos_ref), (ret_hbm, ret_ref), (q_hbm, q_ref),
+                (vhm_hbm, vhm_ref), (v_hbm, v_ref), (k_hbm, k_ref),
+            )
+        )
+    ]
+    for move in moves:
+        move.start()
+    dqc[...] = jnp.zeros_like(dqc)
+    dk_ref[...] = jnp.zeros_like(dk_ref)
+    w_ref[...] = jnp.zeros_like(w_ref)
+    for move in moves[:3]:
+        move.wait()
     rows = base + lax.broadcasted_iota(jnp.int32, (ROWS, 1), 0)
     hits = (rows == pos_ref[...]).astype(jnp.float32)
     count = jnp.sum(hits, axis=1, keepdims=True)
@@ -51,20 +69,22 @@
     slots = lax.broadcasted_iota(jnp.int32, (ROWS, ROWS), 1)
     pick = ((rank.astype(jnp.int32) - 1 == slots) & (marked > 0)).astype(jnp.float32)
     lane = lax.broadcasted_iota(jnp.int32, (ROWS, D), 1)
-    b1 = len_ref[0, 0]
-    b2 = b1 + len_ref[0, 1]
-    b3 = b2 + len_ref[0, 2]
+    b1 = len_ref[:, 0:1]
+    b2 = b1 + len_ref[:, 1:2]
+    b3 = b2 + len_ref[:, 2:3]
     start = jnp.where(rows >= b3, b3, jnp.where(rows >= b2, b2, jnp.where(rows >= b1, b1, 0)))
     fields = jnp.where(lane == 0, count, 0.0)
     fields = jnp.where(lane == 1, total_ret, fields)
     fields = jnp.where(lane == 2, rows.astype(jnp.float32), fields)
     fields = jnp.where(lane == 3, start.astype(jnp.float32), fields)
-    props[...] = tdot(pick, fields, HIGH)
+    props[0:ROWS, :] = tdot(pick, fields, HIGH)
+    props[ROWS:, :] = jnp.zeros((PADDED - ROWS, D), jnp.float32)
     pick_low = pick.astype(jnp.bfloat16)
-    qc[...] = tdot(pick_low, q_ref[...]).astype(jnp.bfloat16)
-    dqc[...] = jnp.zeros_like(dqc)
-    dk_ref[...] = jnp.zeros_like(dk_ref)
-    w_ref[...] = jnp.zeros_like(w_ref)
+    moves[3].wait()
+    qc[0:ROWS, :] = tdot(pick_low, q_ref[...]).astype(jnp.bfloat16)
+    qc[ROWS:, :] = jnp.zeros((PADDED - ROWS, HEADS * D), jnp.bfloat16)
+    for move in moves[4:]:
+        move.wait()
     for c in range(KV):
         readout = jnp.concatenate(
             [vhm_ref[h // 5, h % 5 : h % 5 + 1, :] for h in range(c * GROUP, (c + 1) * GROUP)]
@@ -74,13 +94,13 @@
         rest = readout - high.astype(jnp.float32)
         mid = rest.astype(jnp.bfloat16)
         low = (rest - mid.astype(jnp.float32)).astype(jnp.bfloat16)
-        values = k_ref[:, (KV + c) * D : (KV + c + 1) * D]
+        values = v_ref[:, c * D : (c + 1) * D]
         u_ref[c] = ndot(high, values) + (ndot(mid, values) + ndot(low, values))
     places = (base - 512) + lax.broadcasted_iota(jnp.int32, (1, WIN), 1)
 
     @pl.loop(0, (n + TILE - 1) // TILE)
     def _(t):
-        at = pl.ds(pl.multiple_of(t * TILE, TILE), TILE)
+        at = pl.ds(pl.multiple_of(t * TILE, 16), TILE)
         prop = props[at, :]
         cnt, ret = prop[:, 0:1], prop[:, 1:2]
         row, low = prop[:, 2:3].astype(jnp.int32), prop[:, 3:4].astype(jnp.int32)
@@ -96,7 +116,7 @@
                 h = c * GROUP + g
                 s = jnp.where(allowed, scores[g * TILE : (g + 1) * TILE, :], NEG)
                 e = jnp.exp(s - jnp.max(s, axis=1, keepdims=True))
-                p = e / jnp.sum(e, axis=1, keepdims=True)
+                p = e * (1.0 / jnp.sum(e, axis=1, keepdims=True))
                 probs[h] = p
                 low_p = p.astype(jnp.bfloat16).astype(jnp.float32)
                 hv = jnp.sum(low_p * u_ref[c, g : g + 1, :], axis=1, keepdims=True)
@@ -108,7 +128,7 @@
             q = jnp.concatenate(
                 [qc[at, (c * GROUP + g) * D : (c * GROUP + g + 1) * D] for g in range(GROUP)], axis=0
             )
-            values = k_ref[:, (KV + c) * D : (KV + c + 1) * D]
+            values = v_ref[:, c * D : (c + 1) * D]
             grad_out = jnp.concatenate(
                 [
                     (coef * vhm_ref[h // 5, h % 5 : h % 5 + 1, :]).astype(jnp.bfloat16)
@@ -133,21 +153,29 @@
             dk_ref[:, c * D : (c + 1) * D] += tdot(gs, q) * SCALE
 
     far_ref[...] = dk_ref[: WIN - ROWS, :].astype(jnp.bfloat16)
-    near_ref[...] = dk_ref[WIN - ROWS :, :]
+    moves = [
+        pltpu.make_async_copy(far_ref, far_hbm, sems.at[0]),
+        pltpu.make_async_copy(dk_ref.at[WIN - ROWS :, :], near_hbm, sems.at[1]),
+        pltpu.make_async_copy(w_ref, w_hbm, sems.at[2]),
+    ]
+    for move in moves:
+        move.start()
     dq_ref[...] = jnp.dot(
-        pick_low, dqc[...], preferred_element_type=jnp.float32
+        pick_low, dqc[0:ROWS, :], preferred_element_type=jnp.float32
     ).astype(jnp.bfloat16)
+    for move in moves:
+        move.wait()
 
 
 VMEM = pl.BlockSpec(memory_space=pltpu.VMEM)
-SMEM = pl.BlockSpec(memory_space=pltpu.SMEM)
+ANY = pl.BlockSpec(memory_space=pl.ANY)
 
 
 def shape(dims, kind=jnp.bfloat16):
     return jax.ShapeDtypeStruct(dims, kind)
 
 
-def attention(lengths, positions, returns, queries, keys, vhm):
+def attention(lengths, positions, returns, queries, keys, values, vhm):
     return pl.pallas_call(
         attention_kernel,
         out_shape=(
@@ -156,19 +184,29 @@
             shape((ROWS, KV * D), jnp.float32),
             shape((HEADS, WIN), jnp.float32),
         ),
-        in_specs=[SMEM] + [VMEM] * 5,
-        out_specs=(VMEM,) * 4,
+        in_specs=[ANY] * 7,
+        out_specs=(VMEM, ANY, ANY, ANY),
         scratch_shapes=[
+            pltpu.VMEM((1, 4), jnp.int32),
+            pltpu.VMEM((1, 256), jnp.int32),
+            pltpu.VMEM((1, 256), jnp.float32),
             pltpu.VMEM((ROWS, HEADS * D), jnp.bfloat16),
-            pltpu.VMEM((ROWS, HEADS * D), jnp.bfloat16),
-            pltpu.VMEM((ROWS, D), jnp.float32),
+            pltpu.VMEM((WIN, KV * D), jnp.bfloat16),
+            pltpu.VMEM((WIN, KV * D), jnp.bfloat16),
+            pltpu.VMEM((SP, 8, D), jnp.float32),
+            pltpu.VMEM((PADDED, HEADS * D), jnp.bfloat16),
+            pltpu.VMEM((PADDED, HEADS * D), jnp.bfloat16),
+            pltpu.VMEM((PADDED, D), jnp.float32),
             pltpu.VMEM((HEADS, TILE, WIN), jnp.float32),
             pltpu.VMEM((HEADS, TILE, 1), jnp.float32),
             pltpu.VMEM((WIN, KV * D), jnp.float32),
             pltpu.VMEM((KV, 16, WIN), jnp.float32),
+            pltpu.VMEM((WIN - ROWS, KV * D), jnp.bfloat16),
+            pltpu.VMEM((HEADS, WIN), jnp.float32),
+            pltpu.SemaphoreType.DMA((7,)),
         ],
-        compiler_params=pltpu.CompilerParams(vmem_limit_bytes=48 * 2**20),
-    )(lengths, positions, returns, queries, keys, vhm)
+        compiler_params=pltpu.CompilerParams(vmem_limit_bytes=60 * 2**20),
+    )(lengths, positions, returns, queries, keys, values, vhm)
 
 
 MESH = pl.DeviceIdType.MESH
@@ -238,6 +276,109 @@
             copy.wait_send()
 
 
+class Ring4:
+    def __init__(self, copies, place, axis, view):
+        self.copies, self.view = copies, view
+        self.right, _ = place.along(axis, 1)
+        self.left, _ = place.along(axis, 3)
+        at = getattr(place, axis)
+        self.at = [at, (at + 3) % 4, (at + 1) % 4]
+
+    def send(self, at, half, to):
+        view = self.view(at, half)
+        return self.copies.start(view, view, to)
+
+    def start(self):
+        one, two = slice(0, Z // 2), slice(Z // 2, Z)
+        self.a = [self.send(self.at[0], h, self.right) for h in (one, two)]
+        self.b = [self.send(self.at[0], h, self.left) for h in (two, one)]
+
+    def mid(self):
+        self.a[0].wait_recv()
+        self.c = self.send(self.at[1], slice(0, Z // 2), self.right)
+        self.b[0].wait_recv()
+        self.d = self.send(self.at[2], slice(Z // 2, Z), self.left)
+
+    def end(self):
+        for copy in (self.a[1], self.b[1], self.c, self.d):
+            copy.wait_recv()
+
+
+class Ring8:
+    def __init__(self, copies, place, ref):
+        self.copies, self.ref, self.z = copies, ref, place.z
+        self.right, _ = place.along("z", 1)
+        self.left, _ = place.along("z", Z - 1)
+        self.k = 0
+
+    def send(self, at, half, to):
+        view = self.ref.at[at, half]
+        return self.copies.start(view, view, to)
+
+    def start(self):
+        self.a = [self.send(self.z, h, self.right) for h in (0, 1)]
+        self.b = [self.send(self.z, h, self.left) for h in (1, 0)]
+
+    def step(self):
+        self.k += 1
+        last = self.k == Z // 2 - 1
+        a, b = self.a, self.b
+        self.a, self.b = [], []
+        for i, (right, left) in enumerate(((0, 1), (1, 0))):
+            a[i].wait_recv()
+            if i == 0 or not last:
+                self.a.append(self.send((self.z + Z - self.k) % Z, right, self.right))
+            b[i].wait_recv()
+            if i == 0 or not last:
+                self.b.append(self.send((self.z + self.k) % Z, left, self.left))
+
+    def end(self):
+        for copy in self.a + self.b:
+            copy.wait_recv()
+
+
+def slot(d):
+    return slice((BACK - d) * ROWS, (BACK - d + 1) * ROWS)
+
+
+class Window:
+    def __init__(self, copies, place, ref):
+        x, yl = place.x, place.yl
+        one, two = place.at(x=(x + 1) % X), place.at(x=(x + 2) % X)
+        top, bottom = place.at(yl=1), place.at(yl=0)
+        row = [slot(d) for d in range(BACK + 1)]
+
+        def move(src, dst, to, sends, takes):
+            return copies.make(ref.at[row[src], :], ref.at[row[dst], :], to), sends, takes
+
+        self.m1 = move(0, 1, top, yl == 0, yl == 1)
+        self.m2 = move(0, 2, one, x + 1 < X, x >= 1)
+        self.m4 = move(0, 4, two, x + 2 < X, x >= 2)
+        self.f1 = move(2, 1, bottom, (yl == 1) & (x >= 1), (yl == 0) & (x >= 1))
+        self.f3 = move(2, 3, top, (yl == 0) & (x >= 1), (yl == 1) & (x >= 1))
+        self.g3 = move(4, 3, bottom, (yl == 1) & (x >= 2), (yl == 0) & (x >= 2))
+
+    def start(self):
+        for copy, sends, _ in (self.m2, self.m4, self.m1):
+            pl.when(sends)(copy.start)
+
+    def mid(self):
+        copy, _, takes = self.m2
+        pl.when(takes)(copy.wait_recv)
+        for copy, sends, _ in (self.f1, self.f3):
+            pl.when(sends)(copy.start)
+        copy, _, takes = self.m4
+        pl.when(takes)(copy.wait_recv)
+        copy, sends, _ = self.g3
+        pl.when(sends)(copy.start)
+
+    def end(self):
+        for copy, _, takes in (self.m1, self.f1, self.f3, self.g3):
+            pl.when(takes)(copy.wait_recv)
+        for copy, sends, _ in (self.m1, self.m2, self.m4, self.f1, self.f3, self.g3):
+            pl.when(sends)(copy.wait_send)
+
+
 def greet(place):
     barrier = pltpu.get_barrier_semaphore()
     peers = [place.partner()]
@@ -250,133 +391,159 @@
 
 
 def gather_kernel(
-    t_ref, kv_ref, vhm_ref,
-    kwin, vfull, wb, wg, wa, tb,
-    tsend, pr, pin, ssem, rsem,
+    t_hbm, kv_ref, vhm_ref,
+    kwin, vwin, vfull, wb_hbm, wg_hbm, wa_hbm, tb_hbm,
+    t_ref, wb, wg, wa, tb, tsend, pk, pv, pink, pinv, ssem, rsem, lsem,
 ):
     place = Place()
     copies = Copies(ssem, rsem)
     z, yh, x, yl, core, j = place.z, place.yh, place.x, place.yl, place.core, place.sp
     other = 1 - core
-
-    wb[z, yh, x, yl] = kv_ref[:, 0:384]
-    wg[z, yh, x, yl] = kv_ref[:, 384:768]
-    wa[z, yh, x, yl] = kv_ref[:, 768:1024]
-    vfull[j] = vhm_ref[...]
+    fetch = pltpu.make_async_copy(t_hbm, t_ref, lsem.at[0])
+    fetch.start()
+
+    wb[z, yh, x, yl] = kv_ref[:, 0:256]
+    wg[z, yh, x, yl] = kv_ref[:, 256:512]
+    wa[z, yh, x, yl] = kv_ref[:, 512:1024]
+    vfull[j] = jnp.zeros((8, D), jnp.float32)
+    vfull[j, 0 : HEADS // SP, :] = vhm_ref[...]
     here = pl.ds(pl.multiple_of(core * ROWS, ROWS), ROWS)
     there = pl.ds(pl.multiple_of(other * ROWS, ROWS), ROWS)
+
+    greet(place)
+
+    def spread(axis, view):
+        return [
+            copies.start(view, view, place.along(axis, r)[0]) for r in range(1, COUNT[axis])
+        ]
+
+    def arrive(group):
+        for copy in group:
+            copy.wait_recv()
+
+    a1 = spread("x", wa.at[z, yh, x, yl])
+    b1 = spread("z", wb.at[z, yh, x, yl])
+    g1 = spread("z", wg.at[z, yh, x, yl])
+    v1 = [copies.start(vfull.at[j], vfull.at[j], place.slab(r)) for r in range(1, SP)]
+    b2 = Ring4(copies, place, "y", lambda y, h: wb.at[h, y // YL, x, y % YL])
+    g2 = Ring4(copies, place, "x", lambda x, h: wg.at[h, yh, x, yl])
+    b3 = Ring4(copies, place, "x", lambda x, h: wb.at[h, :, x])
+    g3 = Ring4(copies, place, "y", lambda y, h: wg.at[h, y // YL, :, y % YL])
+    a3 = Ring8(copies, place, wa)
+
+    fetch.wait()
     for b in range(16):
         mine = pl.ds(pl.multiple_of(b * 256 + core * 128, 128), 128)
         theirs = pl.ds(pl.multiple_of(b * 256 + other * 128, 128), 128)
         tb[here, b * 128 : (b + 1) * 128] = t_ref[:, mine]
         tsend[:, b * 128 : (b + 1) * 128] = t_ref[:, theirs]
-
-    greet(place)
-
-    def spread(axis, view):
-        return [
-            copies.start(view, view, place.along(axis, r)[0]) for r in range(1, COUNT[axis])
-        ]
-
-    def arrive(group):
-        for copy in group:
-            copy.wait_recv()
-
-    b1 = spread("z", wb.at[z, yh, x, yl])
-    g1 = spread("z", wg.at[z, yh, x, yl])
-    a1 = spread("x", wa.at[z, yh, x, yl])
-    v1 = [copies.start(vfull.at[j], vfull.at[j], place.slab(r)) for r in range(1, SP)]
     tswap = copies.start(tsend, tb.at[here, :], place.partner())
 
-    arrive(b1)
-    b2 = spread("y", wb.at[:, yh, x, yl])
-    arrive(g1)
-    g2 = spread("x", wg.at[:, yh, x, yl])
     arrive(a1)
     a2 = spread("y", wa.at[z, yh, :, yl])
-    arrive(b2)
-    b3 = spread("x", wb.at[:, :, x, :])
-    arrive(g2)
-    g3 = spread("y", wg.at[:, yh, :, yl])
+    arrive(b1)
+    b2.start()
+    arrive(g1)
+    g2.start()
     arrive(a2)
-    a3 = spread("z", wa.at[z])
-    arrive([tswap])
-    arrive(b3)
-    pr[:, 0:384] = jnp.dot(
-        tb[...], wb[...].reshape(2048, 384), preferred_element_type=jnp.float32
-    )
-    arrive(g3)
-    pr[:, 384:768] = jnp.dot(
-        tb[...], wg[...].reshape(2048, 384), preferred_element_type=jnp.float32
-    )
-    arrive(a3)
-    pr[:, 768:1024] = jnp.dot(
-        tb[...], wa[...].reshape(2048, 256), preferred_element_type=jnp.float32
-    )
-    pswap = copies.start(pr.at[there, :], pin, place.partner())
-    arrive([pswap])
-    own = slice(WIN - ROWS, WIN)
-    kwin[own, :] = (pr[here, :] + pin[...]).astype(jnp.bfloat16)
-    moves = []
+    a3.start()
+    b2.mid()
+    g2.mid()
+    b2.end()
+    b3.start()
+    g2.end()
+    g3.start()
     for d in range(1, BACK + 1):
-        slot = slice((BACK - d) * ROWS, (BACK - d + 1) * ROWS)
-        moves.append(copies.make(kwin.at[own, :], kwin.at[slot, :], place.slab(d)))
-
-        @pl.when(j + d < SP)
-        def _():
-            moves[-1].start()
 
         @pl.when(j - d < 0)
         def _():
-            kwin[slot, :] = jnp.zeros((ROWS, 2 * KV * D), jnp.bfloat16)
-
+            kwin[slot(d), :] = jnp.zeros((ROWS, KV * D), jnp.bfloat16)
+            vwin[slot(d), :] = jnp.zeros((ROWS, KV * D), jnp.bfloat16)
+
+    a3.step()
+    arrive([tswap])
+    b3.mid()
+    g3.mid()
+    a3.step()
+    b3.end()
+    pk[:, 0:256] = jnp.dot(
+        tb[...], wb[...].reshape(2048, 256), preferred_element_type=jnp.float32
+    )
+    g3.end()
+    pk[:, 256:512] = jnp.dot(
+        tb[...], wg[...].reshape(2048, 256), preferred_element_type=jnp.float32
+    )
+    kswap = copies.start(pk.at[there, :], pink, place.partner())
+    a3.step()
+    keep = [
+        pltpu.make_async_copy(src, dst, lsem.at[i])
+        for i, (src, dst) in enumerate(((tb, tb_hbm), (wb, wb_hbm), (wg, wg_hbm), (wa, wa_hbm)))
+    ]
+    for copy in keep[:3]:
+        copy.start()
+    arrive([kswap])
+    kwin[slot(0), :] = (pk[here, :] + pink[...]).astype(jnp.bfloat16)
+    keys, values = Window(copies, place, kwin), Window(copies, place, vwin)
+    keys.start()
+    a3.end()
+    keep[3].start()
+    pv[...] = jnp.dot(tb[...], wa[...].reshape(2048, 512), preferred_element_type=jnp.float32)
+    vswap = copies.start(pv.at[there, :], pinv, place.partner())
+    keys.mid()
+    arrive([vswap])
+    vwin[slot(0), :] = (pv[here, :] + pinv[...]).astype(jnp.bfloat16)
+    values.start()
+    values.mid()
     arrive(v1)
-    for d in range(1, BACK + 1):
-
-        @pl.when(j - d >= 0)
-        def _():
-            moves[d - 1].wait_recv()
-
-        @pl.when(j + d < SP)
-        def _():
-            moves[d - 1].wait_send()
-
+    keys.end()
+    values.end()
     copies.close()
+    for copy in keep:
+        copy.wait()
 
 
 def gather(tokens, kv_weight, vhm):
-    f32 = jnp.float32
+    f32, low = jnp.float32, jnp.bfloat16
     return pl.pallas_call(
         gather_kernel,
         out_shape=(
-            shape((WIN, 2 * KV * D)),
+            shape((WIN, KV * D)),
+            shape((WIN, KV * D)),
             shape((SP, 8, D), f32),
-            shape((Z, YH, X, YL, 16, 384)),
-            shape((Z, YH, X, YL, 16, 384)),
             shape((Z, YH, X, YL, 16, 256)),
+            shape((Z, YH, X, YL, 16, 256)),
+            shape((Z, YH, X, YL, 16, 512)),
             shape((2 * ROWS, 2048)),
         ),
-        in_specs=[VMEM] * 3,
-        out_specs=(VMEM,) * 6,
+        in_specs=[ANY, VMEM, VMEM],
+        out_specs=(VMEM, VMEM, VMEM) + (ANY,) * 4,
         scratch_shapes=[
-            pltpu.VMEM((ROWS, 2048), jnp.bfloat16),
-            pltpu.VMEM((2 * ROWS, 1024), f32),
-            pltpu.VMEM((ROWS, 1024), f32),
-            pltpu.SemaphoreType.DMA((64,)),
-            pltpu.SemaphoreType.DMA((64,)),
+            pltpu.VMEM((ROWS, 4096), low),
+            pltpu.VMEM((Z, YH, X, YL, 16, 256), low),
+            pltpu.VMEM((Z, YH, X, YL, 16, 256), low),
+            pltpu.VMEM((Z, YH, X, YL, 16, 512), low),
+            pltpu.VMEM((2 * ROWS, 2048), low),
+            pltpu.VMEM((ROWS, 2048), low),
+            pltpu.VMEM((2 * ROWS, 512), f32),
+            pltpu.VMEM((2 * ROWS, 512), f32),
+            pltpu.VMEM((ROWS, 512), f32),
+            pltpu.VMEM((ROWS, 512), f32),
+            pltpu.SemaphoreType.DMA((112,)),
+            pltpu.SemaphoreType.DMA((112,)),
+            pltpu.SemaphoreType.DMA((4,)),
         ],
         compiler_params=pltpu.CompilerParams(
-            collective_id=0, has_side_effects=True, vmem_limit_bytes=48 * 2**20
+            collective_id=0, has_side_effects=True, vmem_limit_bytes=60 * 2**20
         ),
     )(tokens, kv_weight, vhm)
 
 
 def reduce_kernel(
-    far_ref, near_ref, w_ref, wb, wg, wa, tb, vfull,
+    far_ref, near_hbm, w_ref, wb_hbm, wg_hbm, wa_hbm, tb_hbm, vfull_hbm,
     ig_ref, wgrad_ref,
-    readout, rk, rw, gk, gw, gb, pb, pg, pa,
+    wb, wg, wa, tb, vfull, readout, rk, rw, gk, gw, gb, pb, pg, pa,
     rb1, rb2, rb3, rg1, rg2, rg3, ra1, ra2, ra3,
-    sb1, sb2, sg1, sg2, sa1, sa2, igs, igr, ssem, rsem,
+    sb1, sb2, sg1, sg2, sa1, sa2, igs, igr, ssem, rsem, lsem,
 ):
     place = Place()
     copies = Copies(ssem, rsem)
@@ -385,39 +552,66 @@
     f32 = jnp.float32
     here = pl.ds(pl.multiple_of(core * ROWS, ROWS), ROWS)
     there = pl.ds(pl.multiple_of(other * ROWS, ROWS), ROWS)
+    copied = (
+        (near_hbm, gk), (w_ref.at[:, WIN - ROWS :], gw), (vfull_hbm, vfull),
+        (tb_hbm, tb), (wb_hbm, wb), (wg_hbm, wg), (wa_hbm, wa),
+    )
+    fetch = [
+        pltpu.make_async_copy(src, dst, lsem.at[i])
+        for i, (src, dst) in enumerate(copied)
+    ]
+    for copy in fetch:
+        copy.start()
     greet(place)
 
-    pairs = []
+    first, second = slice(0, 256), slice(256, 512)
+    streams = [[], [], []]
     for d in range(1, BACK + 1):
-        slot = slice((BACK - d) * ROWS, (BACK - d + 1) * ROWS)
-        pairs.append(
-            (
-                copies.make(far_ref.at[slot, :], rk.at[d - 1], place.slab(SP - d)),
-                copies.make(w_ref.at[:, slot], rw.at[d - 1], place.slab(SP - d)),
-            )
-        )
-
-        @pl.when(j - d >= 0)
-        def _():
-            for copy in pairs[-1]:
-                copy.start()
+        rows, to = slot(d), place.slab(SP - d)
+        streams[0].append(copies.make(w_ref.at[:, rows], rw.at[d - 1], to))
+        for stream, columns in ((streams[1], first), (streams[2], second)):
+            stream.append(copies.make(far_ref.at[rows, columns], rk.at[d - 1, :, columns], to))
+    for stream in streams:
+        for d in range(1, BACK + 1):
+            pl.when(j - d >= 0)(stream[d - 1].start)
+
+    def rest(axis):
+        return range(1, COUNT[axis])
+
+    def add_up(own, slots, n):
+        total = own.astype(f32)
+        for k in range(n):
+            total = total + slots[k].astype(f32)
+        return total
+
+    def swap(columns):
+        view = gb.at[here, columns]
+        return copies.start(view, view, place.partner())
+
+    def keys_arrive(stream, columns):
+        for d in range(1, BACK + 1):
+
+            @pl.when(j + d < SP)
+            def _():
+                stream[d - 1].wait_recv()
+                gk[:, columns] += rk[d - 1, :, columns].astype(f32)
+
+        gb[here, columns] = gk[:, columns].astype(jnp.bfloat16)
+        return swap(columns)
 
     readout[...] = jnp.zeros_like(readout)
+    for copy in fetch[:3]:
+        copy.wait()
     for h in range(HEADS):
         c = h // GROUP
         readout[h : h + 1, c * D : (c + 1) * D] = vfull[h // 5, h % 5 : h % 5 + 1, :]
-    gk[...] = near_ref[...]
-    gw[...] = w_ref[:, WIN - ROWS :]
     for d in range(1, BACK + 1):
 
         @pl.when(j + d < SP)
         def _():
-            for copy in pairs[d - 1]:
-                copy.wait_recv()
-            gk[...] += rk[d - 1].astype(f32)
+            streams[0][d - 1].wait_recv()
             gw[...] += rw[d - 1]
 
-    gb[here, 0:512] = gk[...].astype(jnp.bfloat16)
     whi = gw[...].astype(jnp.bfloat16).astype(f32)
     wlo = gw[...] - whi
     stacked = jnp.concatenate([whi, wlo, jnp.zeros((48, ROWS), f32)], axis=0)
@@ -426,32 +620,10 @@
         gw[...], readout[0:HEADS, :], (((0,), (0,)), ((), ())), precision=HIGH,
         preferred_element_type=f32,
     ).astype(jnp.bfloat16)
-    gswap = copies.start(gb.at[here, :], gb.at[here, :], place.partner())
-    gswap.wait_recv()
-
-    def rest(axis):
-        return range(1, COUNT[axis])
-
-    def add_up(own, slots, n):
-        total = own.astype(f32)
-        for k in range(n):
-            total = total + slots[k].astype(f32)
-        return total
-
-    for n in range(Z):
-        part = tdot(tb[:, n * 256 : (n + 1) * 256], gb[:, 0:256])
-        pb[n] = part.astype(jnp.bfloat16).reshape(YH, X, YL, 16, 256)
-    b1 = []
-    for r in rest("x"):
-        to, at = place.along("x", r)
-        b1.append(copies.start(pb.at[:, :, at], rb1.at[r - 1], to))
-    for n in range(Z):
-        part = tdot(tb[:, n * 256 : (n + 1) * 256], gb[:, 256:512])
-        pg[n] = part.astype(jnp.bfloat16).reshape(YH, X, YL, 16, 256)
-    g1 = []
-    for r in rest("y"):
-        to, at = place.along("y", r)
-        g1.append(copies.start(pg.at[:, at // YL, :, at % YL], rg1.at[r - 1], to))
+    swap_w = swap(slice(512, 1152))
+    for copy in fetch[3:]:
+        copy.wait()
+    swap_w.wait_recv()
     for n in range(Z):
         part = tdot(tb[:, n * 256 : (n + 1) * 256], gb[:, 1024:1152])
         part = part + pltpu.roll(part, 128 - 40, 1)
@@ -460,11 +632,29 @@
     for r in rest("z"):
         to, at = place.along("z", r)
         a1.append(copies.start(pa.at[at], ra1.at[r - 1], to))
-
+    swap_b = keys_arrive(streams[1], first)
+    swap_b.wait_recv()
     for n in range(Z):
-        part = ndot(gb[:, 0:384], wb[n].reshape(256, 384))
-        part = part + ndot(gb[:, 384:768], wg[n].reshape(256, 384))
-        part = part + ndot(gb[:, 768:1024], wa[n].reshape(256, 256))
+        part = tdot(tb[:, n * 256 : (n + 1) * 256], gb[:, 0:256])
+        pb[n] = part.astype(jnp.bfloat16).reshape(YH, X, YL, 16, 256)
+    b1 = []
+    for r in rest("x"):
+        to, at = place.along("x", r)
+        b1.append(copies.start(pb.at[:, :, at], rb1.at[r - 1], to))
+    swap_g = keys_arrive(streams[2], second)
+    swap_g.wait_recv()
+    for n in range(Z):
+        part = tdot(tb[:, n * 256 : (n + 1) * 256], gb[:, 256:512])
+        pg[n] = part.astype(jnp.bfloat16).reshape(YH, X, YL, 16, 256)
+    g1 = []
+    for r in rest("y"):
+        to, at = place.along("y", r)
+        g1.append(copies.start(pg.at[:, at // YL, :, at % YL], rg1.at[r - 1], to))
+
+    for n in range(Z):
+        part = ndot(gb[:, 0:256], wb[n].reshape(256, 256))
+        part = part + ndot(gb[:, 256:512], wg[n].reshape(256, 256))
+        part = part + ndot(gb[:, 512:1024], wa[n].reshape(256, 512))
         igs[:, n * 256 : (n + 1) * 256] = part.astype(jnp.bfloat16)
     iswap = copies.start(igs.at[there, :], igr, place.partner())
 
@@ -534,8 +724,8 @@
 
         @pl.when(j - d >= 0)
         def _():
-            for copy in pairs[d - 1]:
-                copy.wait_send()
+            for stream in streams:
+                stream[d - 1].wait_send()
 
     copies.close()
 
@@ -545,9 +735,14 @@
     return pl.pallas_call(
         reduce_kernel,
         out_shape=(shape((ROWS, 4096)), shape((16, 1024), f32)),
-        in_specs=[VMEM] * 8,
+        in_specs=[ANY] * 8,
         out_specs=(VMEM, VMEM),
         scratch_shapes=[
+            pltpu.VMEM((Z, YH, X, YL, 16, 256), low),
+            pltpu.VMEM((Z, YH, X, YL, 16, 256), low),
+            pltpu.VMEM((Z, YH, X, YL, 16, 512), low),
+            pltpu.VMEM((2 * ROWS, 2048), low),
+            pltpu.VMEM((SP, 8, D), f32),
             pltpu.VMEM((128, KV * D), f32),
             pltpu.VMEM((BACK, ROWS, KV * D), low),
             pltpu.VMEM((BACK, HEADS, ROWS), f32),
@@ -576,17 +771,18 @@
             pltpu.VMEM((ROWS, 2048), low),
             pltpu.SemaphoreType.DMA((64,)),
             pltpu.SemaphoreType.DMA((64,)),
+            pltpu.SemaphoreType.DMA((7,)),
         ],
         compiler_params=pltpu.CompilerParams(
-            collective_id=1, has_side_effects=True, vmem_limit_bytes=56 * 2**20
+            collective_id=1, has_side_effects=True, vmem_limit_bytes=60 * 2**20
         ),
     )(far, near, w, wb, wg, wa, tb, vfull)
 
 
 def on_device(tokens, queries, kv_weight, vhm, lengths, positions, returns):
-    vhm = jnp.pad(vhm.reshape(HEADS // SP, D), ((0, 8 - HEADS // SP), (0, 0)))
-    kwin, vfull, wb, wg, wa, tb = gather(tokens, kv_weight, vhm)
-    dq, far, near, w = attention(lengths, positions, returns, queries, kwin, vfull)
+    vhm = vhm.reshape(HEADS // SP, D)
+    kwin, vwin, vfull, wb, wg, wa, tb = gather(tokens, kv_weight, vhm)
+    dq, far, near, w = attention(lengths, positions, returns, queries, kwin, vwin, vfull)
     input_grad, weight_grad = reduce(far, near, w, wb, wg, wa, tb, vfull)
     return dq, input_grad, weight_grad
 

time: 154 us -> 124 us (0.81)
  Pallas kernels: 140 us -> 120 us
  local copies, waits for them, and re-layouts: 13 us -> 2.95 us
    pallas_call x1, Pallas kernels: 65.4 us -> 52 us  [gather(): pl.pallas_call(gather_kernel, out_shape=(shape((WIN, KV * D)), shape((WIN...]
    unnamed x30 -> x4, local copies, waits for them, and re-layouts: 12.4 us -> 2.95 us
    pallas_call x1, Pallas kernels: 66.1 us -> 56.7 us  [reduce(): pl.pallas_call(reduce_kernel, out_shape=(shape((ROWS, 4096)), shape((16,...]
    pallas_call x1, Pallas kernels: 8.05 us -> 11.2 us  [attention(): pl.pallas_call(attention_kernel, out_shape=(shape((ROWS, HEADS * D)), sha...]
where the time goes in v3:
time: 124 us; the launch traced here: 123 us
  Pallas kernels  120 us (97%)
  local copies, waits for them, and re-layouts  2.95 us (2%)
    pallas_call x1, Pallas kernels, reduce(): pl.pallas_call(reduce_kernel, out_shape=(shape((ROWS, 4096)), shape((16,...  56.7 us
    pallas_call x1, Pallas kernels, gather(): pl.pallas_call(gather_kernel, out_shape=(shape((WIN, KV * D)), shape((WIN...  52 us
    pallas_call x1, Pallas kernels, attention(): pl.pallas_call(attention_kernel, out_shape=(shape((ROWS, HEADS * D)), sha...  11.2 us
    unnamed x4, local copies, waits for them, and re-layouts  2.95 us

profile of v3, /device:TPU:1, one launch (start us, length us, event | category | flops | bytes accessed | tf_op | source)
XLA Modules:
  0.0 123.5 jit_solution(3529397408184127371)
XLA Ops:
  0.6 52.0 %shard_map.94 = (bf16[640,512]{1,0:T(8,128)(2,1)}, bf16[640,512]{1,0:T(8,128)(2,1)}, f32[8,8,128]{2,1,0:T(8,128)}, bf16[8,2,4,2,16,256]{5,4,3,2,1,0:T(8,128)(2,1...) custom-call(bf16[128,4096]{1,0:T(8,128)(2,1)} %t_hbm.1, ...), custom_call_target="tpu_custom_call" | custom-call | tf_op jit(solution)/shard_map/pallas_call | solution.py:507
  52.6 11.2 %shard_map.95 = (bf16[128,5120]{1,0:T(8,128)(2,1)}, bf16[512,512]{1,0:T(8,128)(2,1)}, f32[128,512]{1,0:T(8,128)}, f32[40,640]{1,0:T(8,128)}) custom-call(s32[1,4]{1,0:T(1,128)} %len_hbm.1, s32[1,256]{1,0:T(1,128)} %pos_hbm.1, f32[1,256]{1,0:T(1,128)} %ret_hbm.1, bf16[128,5120]{1,0:T(8,128)(2,1)} %q_hbm.1, bf16[640,512]{1,0:T(8,128)(2,1)} %get-tuple-element.16.k_hbm, ...), custom_call_target="tpu_custom_call" | custom-call | tf_op jit(solution)/shard_map/pallas_call | solution.py:179
  63.8 56.7 %shard_map.96 = (bf16[128,4096]{1,0:T(8,128)(2,1)}, f32[16,1024]{1,0:T(8,128)}) custom-call(bf16[512,512]{1,0:T(8,128)(2,1)} %get-tuple-element.20.far_ref, f32[128,512]{1,0:T(8,128)} %get-tuple-element.21.near_hbm, f32[40,640]{1,0:T(8,128)} %get-tuple-element.22.w_ref, bf16[8,2,4,2,16,256]{5,4,3,2,1,0:T(8,128)(2,1)} %get-tuple-element.23.wb_hbm, ...), custom_call_target="tpu_custom_call" | custom-call | tf_op jit(solution)/shard_map/pallas_call | solution.py:735
  120.5 0.0 copy-start
  120.5 2.3 %copy.12 = bf16[128,4096]{1,0:T(8,128)(2,1)} copy(bf16[128,4096]{1,0:T(8,128)(2,1)} %get-tuple-element.33) | data formatting | bytes 2097152
  122.8 0.0 copy-done
  122.8 0.6 copy.13
Async XLA Ops:
  120.5 2.3 %copy-start = (f32[16,1024]{1,0:T(8,128)S(1)}, f32[16,1024]{1,0:T(8,128)}, u32[]{:S(2)}) copy-start(f32[16,1024]{1,0:T(8,128)} %get-tuple-element.34) | copy-start | bytes 196612

commit v4 on v3

--- a/solution.py
+++ b/solution.py
@@ -390,10 +390,67 @@
     pl.semaphore_wait(barrier, len(peers))
 
 
+class Return:
+    def __init__(self, copies, place, out, have, by_y, by_x, sum2, sum4, total, columns):
+        x, yl = place.x, place.yl
+        self.x, self.yl, self.have = x, yl, have
+        self.total = total.at[:, columns]
+        self.ya, self.yb = by_y.at[0, :, columns], by_y.at[1, :, columns]
+        self.xa, self.xb = by_x.at[0, :, columns], by_x.at[1, :, columns]
+        self.sum2, self.sum4 = sum2.at[:, columns], sum4.at[:, columns]
+        across = place.at(yl=1 - yl)
+        one, two = place.at(x=(x + X - 1) % X), place.at(x=(x + X - 2) % X)
+        self.top, self.bottom = yl == 1, yl == 0
+        self.a = copies.make(out(1), self.ya, across)
+        self.b = copies.make(out(3), self.yb, across)
+        self.c = copies.make(self.sum2, self.xa, one)
+        self.d = copies.make(self.sum4, self.xb, two)
+        self.a_sends = self.top | (x >= 1)
+        self.b_sends = (self.top & (x >= 1)) | (self.bottom & (x >= 2))
+        self.b_takes = (self.bottom & (x >= 1)) | (self.top & (x >= 2))
+        self.a_takes = self.bottom | (x >= 1)
+
+    def start(self):
+        pl.when(self.a_sends)(self.a.start)
+        pl.when(self.b_sends)(self.b.start)
+
+    def add(self, condition, to, what):
+        @pl.when(condition)
+        def _():
+            to[...] = (to[...].astype(jnp.float32) + what[...].astype(jnp.float32)).astype(to.dtype)
+
+    def mid(self):
+        x = self.x
+        self.sum2[...] = self.have(2)[...]
+        self.sum4[...] = self.have(4)[...]
+        pl.when(self.a_takes)(self.a.wait_recv)
+        pl.when(self.b_takes)(self.b.wait_recv)
+        self.add(self.bottom & (x >= 1), self.sum2, self.yb)
+        self.add(self.top & (x >= 1), self.sum2, self.ya)
+        self.add(self.top & (x >= 2), self.sum4, self.yb)
+        self.add(self.bottom, self.total, self.ya)
+        pl.when(x >= 1)(self.c.start)
+        pl.when(x >= 2)(self.d.start)
+
+    def end(self):
+        x = self.x
+        pl.when(x + 1 < X)(self.c.wait_recv)
+        self.add(x + 1 < X, self.total, self.xa)
+        pl.when(x + 2 < X)(self.d.wait_recv)
+        self.add(x + 2 < X, self.total, self.xb)
+
+    def close(self):
+        x = self.x
+        pl.when(self.a_sends)(self.a.wait_send)
+        pl.when(self.b_sends)(self.b.wait_send)
+        pl.when(x >= 1)(self.c.wait_send)
+        pl.when(x >= 2)(self.d.wait_send)
+
+
 def gather_kernel(
     t_hbm, kv_ref, vhm_ref,
-    kwin, vwin, vfull, wb_hbm, wg_hbm, wa_hbm, tb_hbm,
-    t_ref, wb, wg, wa, tb, tsend, pk, pv, pink, pinv, ssem, rsem, lsem,
+    kwin, vwin, vfull, wb_hbm, wg_hbm, wa_hbm, wd_hbm, tb_hbm,
+    t_ref, wb, wg, wa, wd, tb, tsend, pk, pv, pink, pinv, ssem, rsem, lsem,
 ):
     place = Place()
     copies = Copies(ssem, rsem)
@@ -404,7 +461,8 @@
 
     wb[z, yh, x, yl] = kv_ref[:, 0:256]
     wg[z, yh, x, yl] = kv_ref[:, 256:512]
-    wa[z, yh, x, yl] = kv_ref[:, 512:1024]
+    wa[z, yh, x, yl] = kv_ref[:, 512:896]
+    wd[z, yh, x, yl] = kv_ref[:, 896:1024]
     vfull[j] = jnp.zeros((8, D), jnp.float32)
     vfull[j, 0 : HEADS // SP, :] = vhm_ref[...]
     here = pl.ds(pl.multiple_of(core * ROWS, ROWS), ROWS)
@@ -424,11 +482,11 @@
     a1 = spread("x", wa.at[z, yh, x, yl])
     b1 = spread("z", wb.at[z, yh, x, yl])
     g1 = spread("z", wg.at[z, yh, x, yl])
+    d1 = spread("z", wd.at[z, yh, x, yl])
     v1 = [copies.start(vfull.at[j], vfull.at[j], place.slab(r)) for r in range(1, SP)]
-    b2 = Ring4(copies, place, "y", lambda y, h: wb.at[h, y // YL, x, y % YL])
-    g2 = Ring4(copies, place, "x", lambda x, h: wg.at[h, yh, x, yl])
     b3 = Ring4(copies, place, "x", lambda x, h: wb.at[h, :, x])
     g3 = Ring4(copies, place, "y", lambda y, h: wg.at[h, y // YL, :, y % YL])
+    d3 = Ring4(copies, place, "y", lambda y, h: wd.at[h, y // YL, :, y % YL])
     a3 = Ring8(copies, place, wa)
 
     fetch.wait()
@@ -442,17 +500,18 @@
     arrive(a1)
     a2 = spread("y", wa.at[z, yh, :, yl])
     arrive(b1)
-    b2.start()
+    b2 = spread("y", wb.at[:, yh, x, yl])
     arrive(g1)
-    g2.start()
+    g2 = spread("x", wg.at[:, yh, x, yl])
     arrive(a2)
     a3.start()
-    b2.mid()
-    g2.mid()
-    b2.end()
+    arrive(d1)
+    d2 = spread("x", wd.at[:, yh, x, yl])
+    arrive(b2)
     b3.start()
-    g2.end()
+    arrive(g2)
     g3.start()
+    arrive(d2)
     for d in range(1, BACK + 1):
 
         @pl.when(j - d < 0)
@@ -464,6 +523,7 @@
     arrive([tswap])
     b3.mid()
     g3.mid()
+    d3.start()
     a3.step()
     b3.end()
     pk[:, 0:256] = jnp.dot(
@@ -474,10 +534,11 @@
         tb[...], wg[...].reshape(2048, 256), preferred_element_type=jnp.float32
     )
     kswap = copies.start(pk.at[there, :], pink, place.partner())
+    d3.mid()
     a3.step()
     keep = [
         pltpu.make_async_copy(src, dst, lsem.at[i])
-        for i, (src, dst) in enumerate(((tb, tb_hbm), (wb, wb_hbm), (wg, wg_hbm), (wa, wa_hbm)))
+        for i, (src, dst) in enumerate(((tb, tb_hbm), (wb, wb_hbm), (wg, wg_hbm), (wa, wa_hbm), (wd, wd_hbm)))
     ]
     for copy in keep[:3]:
         copy.start()
@@ -485,9 +546,16 @@
     kwin[slot(0), :] = (pk[here, :] + pink[...]).astype(jnp.bfloat16)
     keys, values = Window(copies, place, kwin), Window(copies, place, vwin)
     keys.start()
+    d3.end()
+    keep[4].start()
+    pv[:, 384:512] = jnp.dot(
+        tb[...], wd[...].reshape(2048, 128), preferred_element_type=jnp.float32
+    )
     a3.end()
     keep[3].start()
-    pv[...] = jnp.dot(tb[...], wa[...].reshape(2048, 512), preferred_element_type=jnp.float32)
+    pv[:, 0:384] = jnp.dot(
+        tb[...], wa[...].reshape(2048, 384), preferred_element_type=jnp.float32
+    )
     vswap = copies.start(pv.at[there, :], pinv, place.partner())
     keys.mid()
     arrive([vswap])
@@ -512,16 +580,18 @@
             shape((SP, 8, D), f32),
             shape((Z, YH, X, YL, 16, 256)),
             shape((Z, YH, X, YL, 16, 256)),
-            shape((Z, YH, X, YL, 16, 512)),
+            shape((Z, YH, X, YL, 16, 384)),
+            shape((Z, YH, X, YL, 16, 128)),
             shape((2 * ROWS, 2048)),
         ),
         in_specs=[ANY, VMEM, VMEM],
-        out_specs=(VMEM, VMEM, VMEM) + (ANY,) * 4,
+        out_specs=(VMEM, VMEM, VMEM) + (ANY,) * 5,
         scratch_shapes=[
             pltpu.VMEM((ROWS, 4096), low),
             pltpu.VMEM((Z, YH, X, YL, 16, 256), low),
             pltpu.VMEM((Z, YH, X, YL, 16, 256), low),
-            pltpu.VMEM((Z, YH, X, YL, 16, 512), low),
+            pltpu.VMEM((Z, YH, X, YL, 16, 384), low),
+            pltpu.VMEM((Z, YH, X, YL, 16, 128), low),
             pltpu.VMEM((2 * ROWS, 2048), low),
             pltpu.VMEM((ROWS, 2048), low),
             pltpu.VMEM((2 * ROWS, 512), f32),
@@ -530,7 +600,7 @@
             pltpu.VMEM((ROWS, 512), f32),
             pltpu.SemaphoreType.DMA((112,)),
             pltpu.SemaphoreType.DMA((112,)),
-            pltpu.SemaphoreType.DMA((4,)),
+            pltpu.SemaphoreType.DMA((5,)),
         ],
         compiler_params=pltpu.CompilerParams(
             collective_id=0, has_side_effects=True, vmem_limit_bytes=60 * 2**20
@@ -539,9 +609,9 @@
 
 
 def reduce_kernel(
-    far_ref, near_hbm, w_ref, wb_hbm, wg_hbm, wa_hbm, tb_hbm, vfull_hbm,
+    far_ref, near_hbm, w_ref, wb_hbm, wg_hbm, wa_hbm, wd_hbm, tb_hbm, vfull_hbm,
     ig_ref, wgrad_ref,
-    wb, wg, wa, tb, vfull, readout, rk, rw, gk, gw, gb, pb, pg, pa,
+    wb, wg, wa, wd, tb, vfull, far, wfar, readout, ky, kx, k2, k4, wy, wx, w2, w4, gk, gw, gb, pb, pg, pa,
     rb1, rb2, rb3, rg1, rg2, rg3, ra1, ra2, ra3,
     sb1, sb2, sg1, sg2, sa1, sa2, igs, igr, ssem, rsem, lsem,
 ):
@@ -554,7 +624,8 @@
     there = pl.ds(pl.multiple_of(other * ROWS, ROWS), ROWS)
     copied = (
         (near_hbm, gk), (w_ref.at[:, WIN - ROWS :], gw), (vfull_hbm, vfull),
-        (tb_hbm, tb), (wb_hbm, wb), (wg_hbm, wg), (wa_hbm, wa),
+        (far_ref, far), (w_ref, wfar),
+        (tb_hbm, tb), (wb_hbm, wb), (wg_hbm, wg), (wa_hbm, wa), (wd_hbm, wd),
     )
     fetch = [
         pltpu.make_async_copy(src, dst, lsem.at[i])
@@ -565,15 +636,25 @@
     greet(place)
 
     first, second = slice(0, 256), slice(256, 512)
-    streams = [[], [], []]
-    for d in range(1, BACK + 1):
-        rows, to = slot(d), place.slab(SP - d)
-        streams[0].append(copies.make(w_ref.at[:, rows], rw.at[d - 1], to))
-        for stream, columns in ((streams[1], first), (streams[2], second)):
-            stream.append(copies.make(far_ref.at[rows, columns], rk.at[d - 1, :, columns], to))
+    everything = slice(None)
+    streams = [
+        Return(
+            copies, place,
+            lambda d: w_ref.at[:, slot(d)], lambda d: wfar.at[:, slot(d)], wy, wx, w2, w4, gw,
+            everything,
+        )
+    ]
+    for columns in (first, second):
+        streams.append(
+            Return(
+                copies, place,
+                lambda d, columns=columns: far_ref.at[slot(d), columns],
+                lambda d, columns=columns: far.at[slot(d), columns],
+                ky, kx, k2, k4, gk, columns,
+            )
+        )
     for stream in streams:
-        for d in range(1, BACK + 1):
-            pl.when(j - d >= 0)(stream[d - 1].start)
+        stream.start()
 
     def rest(axis):
         return range(1, COUNT[axis])
@@ -589,29 +670,21 @@
         return copies.start(view, view, place.partner())
 
     def keys_arrive(stream, columns):
-        for d in range(1, BACK + 1):
-
-            @pl.when(j + d < SP)
-            def _():
-                stream[d - 1].wait_recv()
-                gk[:, columns] += rk[d - 1, :, columns].astype(f32)
-
+        stream.end()
         gb[here, columns] = gk[:, columns].astype(jnp.bfloat16)
         return swap(columns)
 
     readout[...] = jnp.zeros_like(readout)
-    for copy in fetch[:3]:
+    for copy in fetch[2:3]:
         copy.wait()
     for h in range(HEADS):
         c = h // GROUP
         readout[h : h + 1, c * D : (c + 1) * D] = vfull[h // 5, h % 5 : h % 5 + 1, :]
-    for d in range(1, BACK + 1):
-
-        @pl.when(j + d < SP)
-        def _():
-            streams[0][d - 1].wait_recv()
-            gw[...] += rw[d - 1]
-
+    for copy in fetch[0:2] + fetch[3:5]:
+        copy.wait()
+    for stream in streams:
+        stream.mid()
+    streams[0].end()
     whi = gw[...].astype(jnp.bfloat16).astype(f32)
     wlo = gw[...] - whi
     stacked = jnp.concatenate([whi, wlo, jnp.zeros((48, ROWS), f32)], axis=0)
@@ -621,7 +694,7 @@
         preferred_element_type=f32,
     ).astype(jnp.bfloat16)
     swap_w = swap(slice(512, 1152))
-    for copy in fetch[3:]:
+    for copy in fetch[5:]:
         copy.wait()
     swap_w.wait_recv()
     for n in range(Z):
@@ -654,7 +727,8 @@
     for n in range(Z):
         part = ndot(gb[:, 0:256], wb[n].reshape(256, 256))
         part = part + ndot(gb[:, 256:512], wg[n].reshape(256, 256))
-        part = part + ndot(gb[:, 512:1024], wa[n].reshape(256, 512))
+        part = part + ndot(gb[:, 512:896], wa[n].reshape(256, 384))
+        part = part + ndot(gb[:, 896:1024], wd[n].reshape(256, 128))
         igs[:, n * 256 : (n + 1) * 256] = part.astype(jnp.bfloat16)
     iswap = copies.start(igs.at[there, :], igr, place.partner())
 
@@ -720,32 +794,36 @@
     wgrad_ref[:, 512:1024] = jnp.dot(
         last, readout[...], precision=HIGH, preferred_element_type=f32
     )
-    for d in range(1, BACK + 1):
-
-        @pl.when(j - d >= 0)
-        def _():
-            for stream in streams:
-                stream[d - 1].wait_send()
-
+    for stream in streams:
+        stream.close()
     copies.close()
 
 
-def reduce(far, near, w, wb, wg, wa, tb, vfull):
+def reduce(far, near, w, wb, wg, wa, wd, tb, vfull):
     f32, low = jnp.float32, jnp.bfloat16
     return pl.pallas_call(
         reduce_kernel,
         out_shape=(shape((ROWS, 4096)), shape((16, 1024), f32)),
-        in_specs=[ANY] * 8,
+        in_specs=[ANY] * 9,
         out_specs=(VMEM, VMEM),
         scratch_shapes=[
             pltpu.VMEM((Z, YH, X, YL, 16, 256), low),
             pltpu.VMEM((Z, YH, X, YL, 16, 256), low),
-            pltpu.VMEM((Z, YH, X, YL, 16, 512), low),
+            pltpu.VMEM((Z, YH, X, YL, 16, 384), low),
+            pltpu.VMEM((Z, YH, X, YL, 16, 128), low),
             pltpu.VMEM((2 * ROWS, 2048), low),
             pltpu.VMEM((SP, 8, D), f32),
+            pltpu.VMEM((WIN - ROWS, KV * D), low),
+            pltpu.VMEM((HEADS, WIN), f32),
             pltpu.VMEM((128, KV * D), f32),
-            pltpu.VMEM((BACK, ROWS, KV * D), low),
-            pltpu.VMEM((BACK, HEADS, ROWS), f32),
+            pltpu.VMEM((2, ROWS, KV * D), low),
+            pltpu.VMEM((2, ROWS, KV * D), low),
+            pltpu.VMEM((ROWS, KV * D), low),
+            pltpu.VMEM((ROWS, KV * D), low),
+            pltpu.VMEM((2, HEADS, ROWS), f32),
+            pltpu.VMEM((2, HEADS, ROWS), f32),
+            pltpu.VMEM((HEADS, ROWS), f32),
+            pltpu.VMEM((HEADS, ROWS), f32),
             pltpu.VMEM((ROWS, KV * D), f32),
             pltpu.VMEM((HEADS, ROWS), f32),
             pltpu.VMEM((2 * ROWS, 1152), low),
@@ -771,19 +849,19 @@
             pltpu.VMEM((ROWS, 2048), low),
             pltpu.SemaphoreType.DMA((64,)),
             pltpu.SemaphoreType.DMA((64,)),
-            pltpu.SemaphoreType.DMA((7,)),
+            pltpu.SemaphoreType.DMA((10,)),
         ],
         compiler_params=pltpu.CompilerParams(
             collective_id=1, has_side_effects=True, vmem_limit_bytes=60 * 2**20
         ),
-    )(far, near, w, wb, wg, wa, tb, vfull)
+    )(far, near, w, wb, wg, wa, wd, tb, vfull)
 
 
 def on_device(tokens, queries, kv_weight, vhm, lengths, positions, returns):
     vhm = vhm.reshape(HEADS // SP, D)
-    kwin, vwin, vfull, wb, wg, wa, tb = gather(tokens, kv_weight, vhm)
+    kwin, vwin, vfull, wb, wg, wa, wd, tb = gather(tokens, kv_weight, vhm)
     dq, far, near, w = attention(lengths, positions, returns, queries, kwin, vwin, vfull)
-    input_grad, weight_grad = reduce(far, near, w, wb, wg, wa, tb, vfull)
+    input_grad, weight_grad = reduce(far, near, w, wb, wg, wa, wd, tb, vfull)
     return dq, input_grad, weight_grad
 
 

time: 124 us -> 119 us (0.960)
  Pallas kernels: 120 us -> 115 us
    pallas_call x1, Pallas kernels: 56.7 us -> 53.3 us  [reduce(): pl.pallas_call(reduce_kernel, out_shape=(shape((ROWS, 4096)), shape((16,...]
    pallas_call x1, Pallas kernels: 52 us -> 50.4 us  [gather(): pl.pallas_call(gather_kernel, out_shape=(shape((WIN, KV * D)), shape((WIN...]
where the time goes in v4:
time: 119 us; the launch traced here: 118 us
  Pallas kernels  115 us (97%)
  local copies, waits for them, and re-layouts  2.95 us (2%)
    pallas_call x1, Pallas kernels, reduce(): pl.pallas_call(reduce_kernel, out_shape=(shape((ROWS, 4096)), shape((16,...  53.3 us
    pallas_call x1, Pallas kernels, gather(): pl.pallas_call(gather_kernel, out_shape=(shape((WIN, KV * D)), shape((WIN...  50.4 us
    pallas_call x1, Pallas kernels, attention(): pl.pallas_call(attention_kernel, out_shape=(shape((ROWS, HEADS * D)), sha...  11.2 us
    unnamed x4, local copies, waits for them, and re-layouts  2.95 us

profile of v4, /device:TPU:1, one launch (start us, length us, event | category | flops | bytes accessed | tf_op | source)
XLA Modules:
  0.0 118.5 jit_solution(15678327527165291414)
XLA Ops:
  0.6 50.4 %shard_map.94 = (bf16[640,512]{1,0:T(8,128)(2,1)}, bf16[640,512]{1,0:T(8,128)(2,1)}, f32[8,8,128]{2,1,0:T(8,128)}, bf16[8,2,4,2,16,256]{5,4,3,2,1,0:T(8,128)(2,1...) custom-call(bf16[128,4096]{1,0:T(8,128)(2,1)} %t_hbm.1, ...), custom_call_target="tpu_custom_call" | custom-call | tf_op jit(solution)/shard_map/pallas_call | solution.py:575
  51.0 11.2 %shard_map.95 = (bf16[128,5120]{1,0:T(8,128)(2,1)}, bf16[512,512]{1,0:T(8,128)(2,1)}, f32[128,512]{1,0:T(8,128)}, f32[40,640]{1,0:T(8,128)}) custom-call(s32[1,4]{1,0:T(1,128)} %len_hbm.1, s32[1,256]{1,0:T(1,128)} %pos_hbm.1, f32[1,256]{1,0:T(1,128)} %ret_hbm.1, bf16[128,5120]{1,0:T(8,128)(2,1)} %q_hbm.1, bf16[640,512]{1,0:T(8,128)(2,1)} %get-tuple-element.17.k_hbm, ...), custom_call_target="tpu_custom_call" | custom-call | tf_op jit(solution)/shard_map/pallas_call | solution.py:179
  62.2 53.3 %shard_map.96 = (bf16[128,4096]{1,0:T(8,128)(2,1)}, f32[16,1024]{1,0:T(8,128)}) custom-call(bf16[512,512]{1,0:T(8,128)(2,1)} %get-tuple-element.21.far_ref, f32[128,512]{1,0:T(8,128)} %get-tuple-element.22.near_hbm, f32[40,640]{1,0:T(8,128)} %get-tuple-element.23.w_ref, bf16[8,2,4,2,16,256]{5,4,3,2,1,0:T(8,128)(2,1)} %get-tuple-element.24.wb_hbm, ...), custom_call_target="tpu_custom_call" | custom-call | tf_op jit(solution)/shard_map/pallas_call | solution.py:804
  115.5 0.0 copy-start
  115.5 2.3 %copy.12 = bf16[128,4096]{1,0:T(8,128)(2,1)} copy(bf16[128,4096]{1,0:T(8,128)(2,1)} %get-tuple-element.35) | data formatting | bytes 2097152
  117.9 0.0 copy-done
  117.9 0.6 copy.13
Async XLA Ops:
  115.5 2.3 %copy-start = (f32[16,1024]{1,0:T(8,128)S(1)}, f32[16,1024]{1,0:T(8,128)}, u32[]{:S(2)}) copy-start(f32[16,1024]{1,0:T(8,128)} %get-tuple-element.36) | copy-start | bytes 196612

commit v5 on v4

--- a/solution.py
+++ b/solution.py
@@ -31,21 +31,26 @@
 
 
 def attention_kernel(
-    len_hbm, pos_hbm, ret_hbm, q_hbm, k_hbm, v_hbm, vhm_hbm, dq_ref, far_hbm, near_hbm, w_hbm,
+    len_hbm, pos_hbm, ret_hbm, q_hbm, k_hbm, v_hbm, vhm_hbm, dq_hbm, far_hbm, near_hbm, w_hbm,
     len_ref, pos_ref, ret_ref, q_ref, k_ref, v_ref, vhm_ref,
-    qc, dqc, props, probs, heads, dk_ref, u_ref, far_ref, w_ref, sems,
+    qc, dqc, props, probs, heads, dk_ref, u_ref, far_ref, w_ref, dq_ref, sems, qsems,
 ):
     base = lax.axis_index("sp") * ROWS
     moves = [
         pltpu.make_async_copy(src, dst, sems.at[i])
         for i, (src, dst) in enumerate(
             (
-                (len_hbm, len_ref), (pos_hbm, pos_ref), (ret_hbm, ret_ref), (q_hbm, q_ref),
+                (len_hbm, len_ref), (pos_hbm, pos_ref), (ret_hbm, ret_ref),
                 (vhm_hbm, vhm_ref), (v_hbm, v_ref), (k_hbm, k_ref),
             )
         )
     ]
-    for move in moves:
+    chunks = [slice(c * GROUP * D, (c + 1) * GROUP * D) for c in range(KV)]
+    quest = [
+        pltpu.make_async_copy(q_hbm.at[:, cols], q_ref.at[:, cols], qsems.at[c])
+        for c, cols in enumerate(chunks)
+    ]
+    for move in moves[:3] + quest + moves[3:]:
         move.start()
     dqc[...] = jnp.zeros_like(dqc)
     dk_ref[...] = jnp.zeros_like(dk_ref)
@@ -80,10 +85,11 @@
     props[0:ROWS, :] = tdot(pick, fields, HIGH)
     props[ROWS:, :] = jnp.zeros((PADDED - ROWS, D), jnp.float32)
     pick_low = pick.astype(jnp.bfloat16)
-    moves[3].wait()
-    qc[0:ROWS, :] = tdot(pick_low, q_ref[...]).astype(jnp.bfloat16)
     qc[ROWS:, :] = jnp.zeros((PADDED - ROWS, HEADS * D), jnp.bfloat16)
-    for move in moves[4:]:
+    for c, cols in enumerate(chunks):
+        quest[c].wait()
+        qc[0:ROWS, cols] = tdot(pick_low, q_ref[:, cols]).astype(jnp.bfloat16)
+    for move in moves[3:]:
         move.wait()
     for c in range(KV):
         readout = jnp.concatenate(
@@ -160,9 +166,13 @@
     ]
     for move in moves:
         move.start()
-    dq_ref[...] = jnp.dot(
-        pick_low, dqc[0:ROWS, :], preferred_element_type=jnp.float32
-    ).astype(jnp.bfloat16)
+    for c, cols in enumerate(chunks):
+        dq_ref[:, cols] = jnp.dot(
+            pick_low, dqc[0:ROWS, cols], preferred_element_type=jnp.float32
+        ).astype(jnp.bfloat16)
+        out = pltpu.make_async_copy(dq_ref.at[:, cols], dq_hbm.at[:, cols], qsems.at[c])
+        out.start()
+        moves.append(out)
     for move in moves:
         move.wait()
 
@@ -185,7 +195,7 @@
             shape((HEADS, WIN), jnp.float32),
         ),
         in_specs=[ANY] * 7,
-        out_specs=(VMEM, ANY, ANY, ANY),
+        out_specs=(ANY,) * 4,
         scratch_shapes=[
             pltpu.VMEM((1, 4), jnp.int32),
             pltpu.VMEM((1, 256), jnp.int32),
@@ -203,7 +213,9 @@
             pltpu.VMEM((KV, 16, WIN), jnp.float32),
             pltpu.VMEM((WIN - ROWS, KV * D), jnp.bfloat16),
             pltpu.VMEM((HEADS, WIN), jnp.float32),
-            pltpu.SemaphoreType.DMA((7,)),
+            pltpu.VMEM((ROWS, HEADS * D), jnp.bfloat16),
+            pltpu.SemaphoreType.DMA((6,)),
+            pltpu.SemaphoreType.DMA((4,)),
         ],
         compiler_params=pltpu.CompilerParams(vmem_limit_bytes=60 * 2**20),
     )(lengths, positions, returns, queries, keys, values, vhm)
@@ -342,14 +354,14 @@
 
 
 class Window:
-    def __init__(self, copies, place, ref):
+    def __init__(self, copies, place, ref, columns):
         x, yl = place.x, place.yl
         one, two = place.at(x=(x + 1) % X), place.at(x=(x + 2) % X)
         top, bottom = place.at(yl=1), place.at(yl=0)
         row = [slot(d) for d in range(BACK + 1)]
 
         def move(src, dst, to, sends, takes):
-            return copies.make(ref.at[row[src], :], ref.at[row[dst], :], to), sends, takes
+            return copies.make(ref.at[row[src], columns], ref.at[row[dst], columns], to), sends, takes
 
         self.m1 = move(0, 1, top, yl == 0, yl == 1)
         self.m2 = move(0, 2, one, x + 1 < X, x >= 1)
@@ -544,27 +556,43 @@
         copy.start()
     arrive([kswap])
     kwin[slot(0), :] = (pk[here, :] + pink[...]).astype(jnp.bfloat16)
-    keys, values = Window(copies, place, kwin), Window(copies, place, vwin)
+    keys = Window(copies, place, kwin, slice(None))
+    parts = [slice(384, 512), slice(0, 256), slice(256, 384)]
+    values = [Window(copies, place, vwin, columns) for columns in parts]
     keys.start()
+
+    def swap_values(columns):
+        return copies.start(pv.at[there, columns], pinv.at[:, columns], place.partner())
+
+    def set_values(columns):
+        vwin[slot(0), columns] = (pv[here, columns] + pinv[:, columns]).astype(jnp.bfloat16)
+
     d3.end()
     keep[4].start()
     pv[:, 384:512] = jnp.dot(
         tb[...], wd[...].reshape(2048, 128), preferred_element_type=jnp.float32
     )
+    vswap = swap_values(parts[0])
+    arrive([vswap])
+    set_values(parts[0])
+    values[0].start()
     a3.end()
     keep[3].start()
     pv[:, 0:384] = jnp.dot(
         tb[...], wa[...].reshape(2048, 384), preferred_element_type=jnp.float32
     )
-    vswap = copies.start(pv.at[there, :], pinv, place.partner())
+    vswap = swap_values(slice(0, 384))
     keys.mid()
     arrive([vswap])
-    vwin[slot(0), :] = (pv[here, :] + pinv[...]).astype(jnp.bfloat16)
-    values.start()
-    values.mid()
+    for columns, window in zip(parts[1:], values[1:]):
+        set_values(columns)
+        window.start()
+    for window in values:
+        window.mid()
     arrive(v1)
     keys.end()
-    values.end()
+    for window in values:
+        window.end()
     copies.close()
     for copy in keep:
         copy.wait()
@@ -610,8 +638,8 @@
 
 def reduce_kernel(
     far_ref, near_hbm, w_ref, wb_hbm, wg_hbm, wa_hbm, wd_hbm, tb_hbm, vfull_hbm,
-    ig_ref, wgrad_ref,
-    wb, wg, wa, wd, tb, vfull, far, wfar, readout, ky, kx, k2, k4, wy, wx, w2, w4, gk, gw, gb, pb, pg, pa,
+    ig_hbm, wgrad_ref,
+    ig_ref, wb, wg, wa, wd, tb, vfull, far, wfar, readout, ky, kx, k2, k4, wy, wx, w2, w4, gk, gw, gb, pb, pg, pa,
     rb1, rb2, rb3, rg1, rg2, rg3, ra1, ra2, ra3,
     sb1, sb2, sg1, sg2, sa1, sa2, igs, igr, ssem, rsem, lsem,
 ):
@@ -782,6 +810,8 @@
         theirs = pl.ds(pl.multiple_of(b * 256 + other * 128, 128), 128)
         ig_ref[:, mine] = igs[here, block]
         ig_ref[:, theirs] = igr[:, block]
+    leave = pltpu.make_async_copy(ig_ref, ig_hbm, lsem.at[0])
+    leave.start()
     for copy in b3:
         copy.wait_recv()
     wgrad_ref[:, 0:256] = add_up(sb2[z], rb3, Z - 1)
@@ -797,6 +827,7 @@
     for stream in streams:
         stream.close()
     copies.close()
+    leave.wait()
 
 
 def reduce(far, near, w, wb, wg, wa, wd, tb, vfull):
@@ -805,8 +836,9 @@
         reduce_kernel,
         out_shape=(shape((ROWS, 4096)), shape((16, 1024), f32)),
         in_specs=[ANY] * 9,
-        out_specs=(VMEM, VMEM),
+        out_specs=(ANY, VMEM),
         scratch_shapes=[
+            pltpu.VMEM((ROWS, 4096), low),
             pltpu.VMEM((Z, YH, X, YL, 16, 256), low),
             pltpu.VMEM((Z, YH, X, YL, 16, 256), low),
             pltpu.VMEM((Z, YH, X, YL, 16, 384), low),
@@ -857,12 +889,44 @@
     )(far, near, w, wb, wg, wa, wd, tb, vfull)
 
 
+def hand_over_kernel(a, b, a_out, b_out, a_here, b_here, come, go):
+    moves = [(b, b_here, b_out)]
+    for k in range(4):
+        rows = slice(k * 32, (k + 1) * 32)
+        moves.append((a.at[rows, :], a_here.at[rows, :], a_out.at[rows, :]))
+    ins = [pltpu.make_async_copy(src, here, come.at[k]) for k, (src, here, _) in enumerate(moves)]
+    outs = [pltpu.make_async_copy(here, dst, go.at[k]) for k, (_, here, dst) in enumerate(moves)]
+    for move in ins:
+        move.start()
+    for first, then in zip(ins, outs):
+        first.wait()
+        then.start()
+    for move in outs:
+        move.wait()
+
+
+def hand_over(a, b):
+    return pl.pallas_call(
+        hand_over_kernel,
+        out_shape=(shape(a.shape, a.dtype), shape(b.shape, b.dtype)),
+        in_specs=[ANY, ANY],
+        out_specs=(ANY, ANY),
+        scratch_shapes=[
+            pltpu.VMEM(a.shape, a.dtype),
+            pltpu.VMEM(b.shape, b.dtype),
+            pltpu.SemaphoreType.DMA((5,)),
+            pltpu.SemaphoreType.DMA((5,)),
+        ],
+        compiler_params=pltpu.CompilerParams(vmem_limit_bytes=60 * 2**20),
+    )(a, b)
+
+
 def on_device(tokens, queries, kv_weight, vhm, lengths, positions, returns):
     vhm = vhm.reshape(HEADS // SP, D)
     kwin, vwin, vfull, wb, wg, wa, wd, tb = gather(tokens, kv_weight, vhm)
     dq, far, near, w = attention(lengths, positions, returns, queries, kwin, vwin, vfull)
     input_grad, weight_grad = reduce(far, near, w, wb, wg, wa, wd, tb, vfull)
-    return dq, input_grad, weight_grad
+    return (dq, *hand_over(input_grad, weight_grad))
 
 
 def solution(mesh):

time: 119 us -> 117 us (0.983)
  local copies, waits for them, and re-layouts: 2.95 us -> 0 us
    unnamed x4 -> x0, local copies, waits for them, and re-layouts: 2.95 us -> none
    pallas_call x0 -> x1, Pallas kernels: none -> 2.04 us  [hand_over(): pl.pallas_call(hand_over_kernel, out_shape=(shape(a.shape, a.dtype), shap...]
where the time goes in v5:
time: 117 us
  Pallas kernels  116 us (99%)
    pallas_call x1, Pallas kernels, reduce(): pl.pallas_call(reduce_kernel, out_shape=(shape((ROWS, 4096)), shape((16,...  53.5 us
    pallas_call x1, Pallas kernels, gather(): pl.pallas_call(gather_kernel, out_shape=(shape((WIN, KV * D)), shape((WIN...  49.8 us
    pallas_call x1, Pallas kernels, attention(): pl.pallas_call(attention_kernel, out_shape=(shape((ROWS, HEADS * D)), sha...  10.9 us

profile of v5, /device:TPU:1, one launch (start us, length us, event | category | flops | bytes accessed | tf_op | source)
XLA Modules:
  0.0 117.0 jit_solution(12392682390047224696)
XLA Ops:
  0.6 49.8 %shard_map.94 = (bf16[640,512]{1,0:T(8,128)(2,1)}, bf16[640,512]{1,0:T(8,128)(2,1)}, f32[8,8,128]{2,1,0:T(8,128)}, bf16[8,2,4,2,16,256]{5,4,3,2,1,0:T(8,128)(2,1...) custom-call(bf16[128,4096]{1,0:T(8,128)(2,1)} %t_hbm.1, ...), custom_call_target="tpu_custom_call" | custom-call | tf_op jit(solution)/shard_map/pallas_call | solution.py:603
  50.4 10.9 %shard_map.95 = (bf16[128,5120]{1,0:T(8,128)(2,1)}, bf16[512,512]{1,0:T(8,128)(2,1)}, f32[128,512]{1,0:T(8,128)}, f32[40,640]{1,0:T(8,128)}) custom-call(s32[1,4]{1,0:T(1,128)} %len_hbm.1, s32[1,256]{1,0:T(1,128)} %pos_hbm.1, f32[1,256]{1,0:T(1,128)} %ret_hbm.1, bf16[128,5120]{1,0:T(8,128)(2,1)} %q_hbm.1, bf16[640,512]{1,0:T(8,128)(2,1)} %get-tuple-element.19.k_hbm, ...), custom_call_target="tpu_custom_call" | custom-call | tf_op jit(solution)/shard_map/pallas_call | solution.py:189
  61.3 53.5 %shard_map.96 = (bf16[128,4096]{1,0:T(8,128)(2,1)}, f32[16,1024]{1,0:T(8,128)}) custom-call(bf16[512,512]{1,0:T(8,128)(2,1)} %get-tuple-element.23.far_ref, f32[128,512]{1,0:T(8,128)} %get-tuple-element.24.near_hbm, f32[40,640]{1,0:T(8,128)} %get-tuple-element.25.w_ref, bf16[8,2,4,2,16,256]{5,4,3,2,1,0:T(8,128)(2,1)} %get-tuple-element.26.wb_hbm, ...), custom_call_target="tpu_custom_call" | custom-call | tf_op jit(solution)/shard_map/pallas_call | solution.py:835
  114.8 2.0 %shard_map.97 = (bf16[128,4096]{1,0:T(8,128)(2,1)}, f32[16,1024]{1,0:T(8,128)}) custom-call(bf16[128,4096]{1,0:T(8,128)(2,1)} %get-tuple-element.31.a, f32[16,1024]{1,0:T(8,128)} %get-tuple-element.32.b), custom_call_target="tpu_custom_call" | custom-call | tf_op jit(solution)/shard_map/pallas_call | solution.py:909
